TPU v7x, 256 devices: a whole 4x4x8 slice. The times are simulated.
256 devices in a mesh: row: 8 (over y, z_hi), col: 4 (over x), tok: 8 (over z_lo, core).
Axes of the slice: x: 4, y: 4, z: 8 (z_hi: 2, z_lo: 4; z = z_hi * 4 + z_lo), core: 2. Of those that a mesh axis runs over, the one named last changes fastest.
Arguments:
- first_inputs: bfloat16 [2048, 8192], P(('row', 'col'), 'tok'), may hold values from -12 to 12, as said below
- second_inputs: bfloat16 [2048, 8192], P(('row', 'col'), 'tok'), may hold values from -12 to 12, as said below
- first_weights: bfloat16 [8192, 2, 14336], P('tok', None, ('row', 'col')), may hold values from -0.0625 to 0.0625
- second_weights: bfloat16 [8192, 2, 14336], P('tok', None, ('col', 'row')), may hold values from -0.0625 to 0.0625
Outputs:
- unit_scores: float32 [14336, 14336], P(('row', 'tok'), 'col')
Inputs may be any that keep to these rules, and one draw needn't show every extreme that they name: `first_inputs`: the first model's layer input for each calibration token. `second_inputs`: the second model's layer input for each calibration token.
All inputs are finite; a program needn't handle non-finite values.
Results may differ from a plain program's by a relative error of at most 0.015.
Values may be sent and summed in bfloat16 or wider, within the bound.
No kernel may reach another device: no remote copies, remote signals or barrier semaphores. Data moves between devices by JAX's collectives and lax.ppermute only.
A program may use at most 128 MiB of HBM per device.

v0:
```python
import functools
import itertools

import jax
import jax.numpy as jnp
from jax import lax
from jax.experimental import pallas as pl
from jax.experimental.pallas import tpu as pltpu
from jax.sharding import Mesh, PartitionSpec as P

AXES = ("y", "zh", "x", "a", "b", "c")
SIZES = dict(y=4, zh=2, x=4, a=2, b=2, c=2)


def move(value, axes, target):
    sizes = [SIZES[axis] for axis in axes]
    pairs = []
    for source, place in enumerate(itertools.product(*[range(size) for size in sizes])):
        goal = target(**dict(zip(axes, place)))
        if goal is None:
            continue
        index = 0
        for size, coordinate in zip(sizes, goal):
            index = index * size + coordinate % size
        pairs.append((source, index))
    return lax.ppermute(value, axes, pairs)


def swap(value, axis):
    return move(value, (axis,), lambda **place: (place[axis] + 1,))


MASKS = (0, 1, 3, 2)


def plane(value, stage, mask):
    return move(
        value, ("y", "x", "c"), lambda y, x, c: (y, x ^ mask, c) if c == stage else (y ^ mask, x, c)
    )


def direct(value):
    return value, plane(value, 0, 1), plane(value, 0, 3), plane(value, 0, 2)


def ring(value, cut, *first):
    one = plane(value, 1, 1)
    three = plane(value, 1, 3)
    if first:
        one, three, *first = lax.optimization_barrier((one, three, *first))
    half = value.shape[cut] // 2
    far_low = plane(lax.slice_in_dim(one, 0, half, axis=cut), 1, 3)
    far_high = plane(lax.slice_in_dim(three, half, 2 * half, axis=cut), 1, 1)
    return value, one, three, far_low, far_high, *first


def absolute(value, me, dim):
    shape = value.shape
    value = value.reshape(*shape[:dim], 2, 2, *shape[dim + 1 :])
    low, high = (lax.index_in_dim(value, i, dim) for i in range(2))
    value = jnp.concatenate([low, lax.rev(high, (dim + 1,))], axis=dim)
    value = jnp.where(me % 2 == 0, value, lax.rev(value, (dim + 1,)))
    value = jnp.where(me // 2 == 0, value, lax.rev(value, (dim,)))
    return value.reshape(shape)


def product_kernel(ranges, tiles, count, *refs):
    weights, inputs = refs[:count], refs[count : count + len(ranges)]
    kept_ref, sent_ref, held_weights, held, arrived = refs[count + len(ranges) :]
    width = inputs[0].shape[1]
    pieces, column, row = [], 0, 0
    for ref in weights:
        pieces.append((ref, held_weights.at[:, pl.ds(column, ref.shape[1])]))
        column += ref.shape[1]
    for ref, (start, blocks) in zip(inputs, ranges):
        pieces.append((ref.at[pl.ds(start, blocks)], held.at[pl.ds(row, blocks)]))
        row += blocks
    copies = [pltpu.make_async_copy(*piece, arrived.at[i]) for i, piece in enumerate(pieces)]
    for copy in copies:
        copy.start()
    for copy in copies[:count]:
        copy.wait()
    done, waited = 0, count
    for blocks, needed in tiles:
        for copy in copies[waited : count + needed]:
            copy.wait()
        waited = count + needed
        sums = lax.dot_general(
            held_weights[...],
            held[done : done + blocks].reshape(blocks * width, column),
            (((1,), (1,)), ((), ())),
            preferred_element_type=jnp.float32,
        )
        for i in range(blocks):
            block = sums[:, i * width : (i + 1) * width].reshape(2, *kept_ref.shape[1:])
            kept_ref[done + i] = block[0]
            sent_ref[done + i] = block[1].astype(sent_ref.dtype)
        done += blocks


def called(kernel, out_shape, scratch_shapes, *arrays, scalars=(), space=pltpu.VMEM):
    vmem = pl.BlockSpec(memory_space=pltpu.VMEM)
    return pl.pallas_call(
        kernel,
        out_shape=out_shape,
        in_specs=[pl.BlockSpec(memory_space=pltpu.SMEM)] * len(scalars)
        + [pl.BlockSpec(memory_space=space)] * len(arrays),
        out_specs=jax.tree.map(lambda _: vmem, out_shape),
        scratch_shapes=scratch_shapes,
        compiler_params=pltpu.CompilerParams(vmem_limit_bytes=48 * 1024 * 1024),
        cost_estimate=pl.CostEstimate(flops=1, bytes_accessed=1, transcendentals=0),
    )(*scalars, *arrays)


def products(weights, inputs, ranges, tiles):
    units, count = weights[0].shape[0], sum(blocks for _, blocks in ranges)
    _, width, depth = inputs[0].shape
    shape = (count, 2, units // 4, width)
    return called(
        functools.partial(product_kernel, ranges, tiles, len(weights)),
        (jax.ShapeDtypeStruct(shape, jnp.float32), jax.ShapeDtypeStruct(shape, jnp.bfloat16)),
        [
            pltpu.VMEM((units, depth), weights[0].dtype),
            pltpu.VMEM((count, width, depth), weights[0].dtype),
            pltpu.SemaphoreType.DMA((len(weights) + len(inputs),)),
        ],
        *weights,
        *inputs,
        space=pl.ANY,
    )


def norm_kernel(position_ref, *refs):
    sums, (out_ref, act) = refs[:-2], refs[-2:]
    total = 0.0
    count, _, width = act.shape
    done = 0
    for kept_ref, came_ref in zip(sums[::2], sums[1::2]):
        for i in range(kept_ref.shape[0]):
            gate = kept_ref[i, 0] + came_ref[i, 0].astype(jnp.float32)
            up = kept_ref[i, 1] + came_ref[i, 1].astype(jnp.float32)
            value = gate / (1.0 + jnp.exp(-gate)) * up
            act[done] = value
            total += value
            done += 1
    inverse = 1.0 / (count * width)
    mean = jnp.sum(total, axis=1, keepdims=True) * inverse
    squares = 0.0
    for i in range(count):
        deviation = act[i] - mean
        squares += deviation * deviation
    scale = lax.rsqrt(jnp.sum(squares, axis=1, keepdims=True) * inverse + 1e-05)
    for i in range(count):
        place = pl.multiple_of(position_ref[i] * width, width)
        out_ref[:, pl.ds(place, width)] = ((act[i] - mean) * scale).astype(out_ref.dtype)


def normalized(positions, *sums):
    count = positions.shape[0]
    _, _, units, width = sums[0].shape
    return called(
        norm_kernel,
        jax.ShapeDtypeStruct((units, count * width), jnp.bfloat16),
        [pltpu.VMEM((count, units, width), jnp.float32)],
        *sums,
        scalars=(positions,),
    )


def local(first_inputs, second_inputs, first_weights, second_weights):
    a, b, c, x, y, zh = (lax.axis_index(name) for name in ("a", "b", "c", "x", "y", "zh"))
    depth, _, units = first_weights.shape
    piece = first_inputs.shape[0]
    tokens = piece * 32
    half, quarter, eighth = units // 2, units // 4, units // 8
    is_first = b == 0
    sent_inputs = jnp.where(is_first, second_inputs, first_inputs)
    own_inputs = jnp.where(is_first, first_inputs, second_inputs)
    own_zh = jnp.concatenate([own_inputs, swap(sent_inputs, "b")], axis=1)
    other_zh = jnp.concatenate(
        [swap(own_inputs, "zh"), move(sent_inputs, ("zh", "b"), lambda zh, b: (zh + 1, b + 1))], axis=1
    )

    def turned_weights(model):
        parts = model.transpose(1, 2, 0).reshape(2, 2, half, depth).swapaxes(0, 1)
        return jnp.where(c == 0, parts, lax.rev(parts, (0,))).reshape(2 * units, depth)

    sent_weights = turned_weights(jnp.where(is_first, second_weights, first_weights))
    own_weights = turned_weights(jnp.where(is_first, first_weights, second_weights))
    split = depth * 3 // 8
    came_one, came_two = swap(sent_weights[:, :split], "b"), swap(sent_weights[:, split:], "b")

    block = jnp.concatenate(
        [jnp.where(zh == 0, own_zh, other_zh), jnp.where(zh == 0, other_zh, own_zh)], axis=0
    )
    block, came_one = lax.optimization_barrier((jnp.stack(direct(block)), came_one))
    own, one, three, far_low, far_high, came_two = ring(block, 0, came_two)
    weights = own_weights, came_one, came_two

    def core_sum(kept, sent, order):
        came = swap(sent, "c")
        came = jnp.stack([came[i] for i in order])
        return (kept + came.astype(jnp.float32)).reshape(-1, 2, 2, quarter, 2 * piece)

    def depth_parts(sums):
        sent = lax.dynamic_index_in_dim(sums, 1 - a, 2, keepdims=False).astype(jnp.bfloat16)
        kept = lax.dynamic_index_in_dim(sums, a, 2, keepdims=False)
        return [kept[:, :, :eighth], kept[:, :, eighth:]], [sent[:, :, :eighth], sent[:, :, eighth:]]

    early_blocks = [(i, j) for i in range(3) for j in range(3)]
    late_blocks = [(i, 3) for i in range(3)] + [(3, j) for j in range(4)]
    turned = [[blocks.index((j, i)) for i, j in blocks] for blocks in (early_blocks, late_blocks)]
    early = products(weights, (own, one, three), ((0, 3),) * 3, ((2, 1), (4, 2), (3, 3)))
    early, far_low, far_high = lax.optimization_barrier((early, far_low, far_high))
    early = core_sum(*early, turned[0])
    early, far_low, far_high = lax.optimization_barrier((early, far_low, far_high))
    early, early_came = depth_parts(early)
    early_came = [swap(part, "a") for part in early_came]
    late = products(
        weights,
        (own, one, three, far_low, far_high),
        ((3, 1),) * 3 + ((0, 2),) * 2,
        ((4, 4), (3, 5)),
    )
    late, early_came[0] = lax.optimization_barrier((late, early_came[0]))
    late = core_sum(*late, turned[1])
    late, early_came[1] = lax.optimization_barrier((late, early_came[1]))
    late, late_came = depth_parts(late)
    late_came = [swap(part, "a") for part in late_came]

    first, second = jnp.where(c == 0, x, y), jnp.where(c == 0, y, x)
    positions = []
    for i, j in early_blocks + late_blocks:
        mine, yours = second ^ MASKS[i], first ^ MASKS[j]
        positions.append(jnp.where(c == 0, mine * 4 + yours, yours * 4 + mine))
    positions = jnp.stack(positions)
    norm = [normalized(positions, early[h], early_came[h], late[h], late_came[h]) for h in range(2)]

    two = move(norm[0], ("b",), lambda b: (0,) if b == 1 else None)
    came = [
        move(norm[h], ("x", "a", "b"), lambda x, a, b: (2 * a + h, x // 2, x % 2) if b == 0 else None)
        for h in range(2)
    ]
    one = jnp.where(x % 2 == 0, came[0], came[1])
    two = jnp.where(is_first, two, norm[1])
    two = lax.all_gather(two, ("zh", "a", "b"), axis=0, tiled=True)
    *one, two = ring(jnp.stack(direct(one)), 2, two)
    two_core = swap(two, "c")
    pair = jnp.stack([jnp.where(c == 0, two, two_core), jnp.where(c == 0, two_core, two)])
    pair = pair.reshape(2, 2, half, tokens).transpose(1, 0, 2, 3).reshape(4 * half, tokens)

    *one, pair = lax.optimization_barrier((*one, pair))
    one = jnp.stack([*one[:3], jnp.concatenate(one[3:], axis=2)])

    scores = lax.dot_general(
        one.reshape(4 * half, tokens), pair, (((1,), (1,)), ((), ())), preferred_element_type=jnp.float32
    )
    scores = (scores * float(tokens) ** (-0.5)).astype(jnp.bfloat16).reshape(4, 4, eighth, 4 * half)
    scores = jnp.where(c == 0, scores, scores.swapaxes(0, 1))
    scores = absolute(absolute(scores, y, 0), x, 1).reshape(4, half, 4 * half)
    scores = lax.all_to_all(scores, "y", 0, 0, tiled=True)
    return jnp.concatenate([scores[i] for i in range(4)], axis=1).astype(jnp.float32)


def solution(mesh):
    fine = Mesh(mesh.devices.reshape([SIZES[axis] for axis in AXES]), AXES)
    specs = (
        P(("y", "zh", "x"), ("a", "b", "c")),
        P(("y", "zh", "x"), ("a", "b", "c")),
        P(("a", "b", "c"), None, ("y", "zh", "x")),
        P(("a", "b", "c"), None, ("x", "y", "zh")),
    )
    return jax.shard_map(
        local, mesh=fine, in_specs=specs, out_specs=P(("y", "zh", "a", "b", "c"), "x"), check_vma=False
    )
```

profile of v0, /device:TPU:224, one launch (start us, length us, event | category | flops | bytes accessed | tf_op | source)
XLA Modules:
  0.0 264.5 jit_solution(16765601740286215022)
XLA Ops:
  7.7 1.9 collective-permute-start
  9.6 4.5 %collective-permute-start.1 = (bf16[64,1024]{1,0:T(8,128)(2,1)S(1)}, bf16[64,1024]{1,0:T(8,128)(2,1)S(1)}, u32[]{:S(2)}, u32[]{:S(2)}) collective-permute-start(bf16[64,1024]{1,0:T(8,128)(2,1)S(1)} %get-tuple-element.92), channel_id=1, source_target_pairs={{0,32},{32,0},{1,33},{33,1},{2,34},{34,2},{3,35},{35,3},{4,36},{36... | collective-permute-start | bytes 393224 | tf_op jit(solution)/shard_map/ppermute | solution.py:26
  14.1 3.5 %broadcast_select_fusion.2 = (bf16[1024,2,448]{0,2,1:T(8,128)(2,1)}, bf16[1024,2,448]{0,2,1:T(8,128)(2,1)S(1)}) fusion(bf16[1024,2,448]{0,2,1:T(8,128)(2,1)} %param.7, bf16[1024,2,448]{0,2,1:T(8,128)(2,1)} %param.6, pred[]{:T(512)S(6)} %eq.22), kind=kLoop, calls=%fused_computation.15 | loop fusion | flops 1835008 | bytes 7340033 | tf_op jit(solution)/shard_map/jit(_where)/select_n | solution.py:188
  19.3 2.5 collective-permute-done.1
  23.6 2.1 collective-permute-start.4
  26.9 4.8 %collective-permute-start.6 = (bf16[896,384]{1,0:T(8,128)(2,1)S(1)}, bf16[896,384]{1,0:T(8,128)(2,1)S(1)}, u32[]{:S(2)}, u32[]{:S(2)}) collective-permute-start(bf16[896,384]{1,0:T(8,128)(2,1)S(1)} %slice.147), channel_id=1, source_target_pairs={{0,2},{2,0},{1,3},{3,1},{4,6},{6,4},{5,7},{7,5},{8,10},{10,8},{9,1... | collective-permute-start | bytes 2064392 | tf_op jit(solution)/shard_map/ppermute | solution.py:26
  31.7 7.9 %collective-permute-done.4 = bf16[128,2048]{1,0:T(8,128)(2,1)S(1)} collective-permute-done((bf16[128,2048]{1,0:T(8,128)(2,1)S(1)}, bf16[128,2048]{1,0:T(8,128)(2,1)S(1)}, u32[]{:S(2)}, u32[]{:S(2)}) %collective-permute-start.4) | collective-permute-done | bytes 524320 | tf_op jit(solution)/shard_map/ppermute | solution.py:26
  39.9 7.1 %collective-permute-done.6.refs_1_ = bf16[896,384]{1,0:T(8,128)(2,1)S(1)} collective-permute-done((bf16[896,384]{1,0:T(8,128)(2,1)S(1)}, bf16[896,384]{1,0:T(8,128)(2,1)S(1)}, u32[]{:S(2)}, u32[]{:S(2)}) %collective-permute-start.6) | collective-permute-done | bytes 688160 | tf_op jit(solution)/shard_map/ppermute | solution.py:26
  47.9 2.2 collective-permute-start.8
  52.1 24.6 %collective-permute-done.9.refs_2_ = bf16[896,640]{1,0:T(8,128)(2,1)S(1)} collective-permute-done((bf16[896,640]{1,0:T(8,128)(2,1)S(1)}, bf16[896,640]{1,0:T(8,128)(2,1)S(1)}, u32[]{:S(2)}, u32[]{:S(2)}) %collective-permute-start.9) | collective-permute-done | bytes 1146912 | tf_op jit(solution)/shard_map/ppermute | solution.py:26
  79.7 9.0 %shard_map.46 = (f32[9,2,224,128]{3,2,1,0:T(8,128)}, bf16[9,2,224,128]{3,2,1,0:T(8,128)(2,1)}) custom-call(bf16[896,1024]{1,0:T(8,128)(2,1)S(1)} %bitcast.83, bf16[896,384]{1,0:T(8,128)(2,1)S(1)} %collective-permute-done.6.refs_1_, bf16[896,640]{1,0:T(8,128)(2,1)S(1)} %collective-permute-done.9.refs_2_, bf16[4,128,2048]{2,1,0:T(8,128)(2,1)} %copy-done.7, ...), custom_call_target="tpu_custom_call" | custom-call | flops 1 | bytes 1 | tf_op jit(solution)/shard_map/pallas_call | solution.py:103
  88.8 4.2 %collective-permute-done.10.refs_6_ = bf16[2,128,2048]{2,1,0:T(8,128)(2,1)S(1)} collective-permute-done((bf16[2,128,2048]{2,1,0:T(8,128)(2,1)S(1)}, bf16[2,128,2048]{2,1,0:T(8,128)(2,1)S(1)}, u32[]{:S(2)}, u32[]{:S(2)}) %collective-permute-start.10) | collective-permute-done | bytes 1048608 | tf_op jit(solution)/shard_map/ppermute | solution.py:26
  94.9 2.8 %collective-permute-done.12 = bf16[9,2,224,128]{3,2,1,0:T(8,128)(2,1)S(1)} collective-permute-done((bf16[9,2,224,128]{3,2,1,0:T(8,128)(2,1)}, bf16[9,2,224,128]{3,2,1,0:T(8,128)(2,1)S(1)}, u32[]{:S(2)}, u32[]{:S(2)}) %collective-permute-start.12) | collective-permute-done | bytes 1032224 | tf_op jit(solution)/shard_map/ppermute | solution.py:26
  98.0 1.9 convert_add_fusion
  102.1 7.3 %shard_map.47 = (f32[7,2,224,128]{3,2,1,0:T(8,128)}, bf16[7,2,224,128]{3,2,1,0:T(8,128)(2,1)S(1)}) custom-call(bf16[896,1024]{1,0:T(8,128)(2,1)} %bitcast.84, bf16[896,384]{1,0:T(8,128)(2,1)S(1)} %copy-done.2, bf16[896,640]{1,0:T(8,128)(2,1)S(1)} %collective-permute-done.9.refs_2_, bf16[4,128,2048]{2,1,0:T(8,128)(2,1)} %copy-done.7, ...), custom_call_target="tpu_custom_call" | custom-call | flops 1 | bytes 1 | tf_op jit(solution)/shard_map/pallas_call | solution.py:103
  109.3 5.5 %collective-permute-done.13.refs_1_ = bf16[9,2,56,128]{3,2,1,0:T(8,128)(2,1)S(1)} collective-permute-done((bf16[9,2,56,128]{3,2,1,0:T(8,128)(2,1)S(1)}, bf16[9,2,56,128]{3,2,1,0:T(8,128)(2,1)S(1)}, u32[]{:S(2)}, u32[]{:S(2)}) %collective-permute-start.13) | collective-permute-done | bytes 258080 | tf_op jit(solution)/shard_map/ppermute | solution.py:26
  117.9 10.7 %collective-permute-done.15.refs_1_ = bf16[9,2,56,128]{3,2,1,0:T(8,128)(2,1)S(1)} collective-permute-done((bf16[9,2,56,128]{3,2,1,0:T(8,128)(2,1)S(1)}, bf16[9,2,56,128]{3,2,1,0:T(8,128)(2,1)S(1)}, u32[]{:S(2)}, u32[]{:S(2)}) %collective-permute-start.15) | collective-permute-done | bytes 258080 | tf_op jit(solution)/shard_map/ppermute | solution.py:26
  128.9 12.0 %collective-permute-done.16.refs_3_ = bf16[7,2,56,128]{3,2,1,0:T(8,128)(2,1)S(1)} collective-permute-done((bf16[7,2,56,128]{3,2,1,0:T(8,128)(2,1)S(1)}, bf16[7,2,56,128]{3,2,1,0:T(8,128)(2,1)S(1)}, u32[]{:S(2)}, u32[]{:S(2)}) %collective-permute-start.16) | collective-permute-done | bytes 200736 | tf_op jit(solution)/shard_map/ppermute | solution.py:26
  143.2 2.8 %collective-permute-start.18 = (bf16[7,2,56,128]{3,2,1,0:T(8,128)(2,1)S(1)}, bf16[7,2,56,128]{3,2,1,0:T(8,128)(2,1)S(1)}, u32[]{:S(2)}, u32[]{:S(2)}) collective-permute-start(bf16[7,2,56,128]{3,2,1,0:T(8,128)(2,1)S(1)} %get-tuple-element.89), channel_id=1, source_target_pairs={{0,4},{4,0},{1,5},{5,1},{2,6},{6,2},{3,7},{7,3},{8,12},{12,8},{9,1... | collective-permute-start | bytes 602120 | tf_op jit(solution)/shard_map/ppermute | solution.py:26
  145.9 8.3 %collective-permute-done.18.refs_3_ = bf16[7,2,56,128]{3,2,1,0:T(8,128)(2,1)S(1)} collective-permute-done((bf16[7,2,56,128]{3,2,1,0:T(8,128)(2,1)S(1)}, bf16[7,2,56,128]{3,2,1,0:T(8,128)(2,1)S(1)}, u32[]{:S(2)}, u32[]{:S(2)}) %collective-permute-start.18) | collective-permute-done | bytes 200736 | tf_op jit(solution)/shard_map/ppermute | solution.py:26
  158.0 20.5 %collective-permute-done.17 = bf16[56,2048]{1,0:T(8,128)(2,1)S(1)} collective-permute-done((bf16[56,2048]{1,0:T(8,128)(2,1)S(1)}, bf16[56,2048]{1,0:T(8,128)(2,1)S(1)}, u32[]{:S(2)}, u32[]{:S(2)}) %collective-permute-start.17) | collective-permute-done | bytes 229408 | tf_op jit(solution)/shard_map/ppermute | solution.py:26
  178.6 12.9 %collective-permute-start.21 = (bf16[56,2048]{1,0:T(8,128)(2,1)S(1)}, bf16[56,2048]{1,0:T(8,128)(2,1)S(1)}, u32[]{:S(2)}, u32[]{:S(2)}) collective-permute-start(bf16[56,2048]{1,0:T(8,128)(2,1)S(1)} %broadcast_select_fusion.7), channel_id=1, source_target_pairs={{0,24},{1,193},{8,16},{9,201},{16,8},{17,209},{24,0},{25,217},{64,... | collective-permute-start | bytes 688136 | tf_op jit(solution)/shard_map/ppermute | solution.py:26
  191.5 5.5 %collective-permute-done.21 = bf16[56,2048]{1,0:T(8,128)(2,1)S(1)} collective-permute-done((bf16[56,2048]{1,0:T(8,128)(2,1)S(1)}, bf16[56,2048]{1,0:T(8,128)(2,1)S(1)}, u32[]{:S(2)}, u32[]{:S(2)}) %collective-permute-start.21) | collective-permute-done | bytes 229408 | tf_op jit(solution)/shard_map/ppermute | solution.py:26
  197.0 2.7 %collective-permute-done.22 = bf16[56,2048]{1,0:T(8,128)(2,1)S(1)} collective-permute-done((bf16[56,2048]{1,0:T(8,128)(2,1)S(1)}, bf16[56,2048]{1,0:T(8,128)(2,1)S(1)}, u32[]{:S(2)}, u32[]{:S(2)}) %collective-permute-start.22) | collective-permute-done | bytes 229408 | tf_op jit(solution)/shard_map/ppermute | solution.py:26
  201.8 11.5 %collective-permute-done.23 = bf16[4,56,2048]{2,1,0:T(8,128)(2,1)S(1)} collective-permute-done((bf16[4,56,2048]{2,1,0:T(8,128)(2,1)S(1)}, bf16[4,56,2048]{2,1,0:T(8,128)(2,1)S(1)}, u32[]{:S(2)}, u32[]{:S(2)}) %collective-permute-start.23) | collective-permute-done | bytes 917536 | tf_op jit(solution)/shard_map/ppermute | solution.py:26
  214.7 1.8 collective-permute-start.26
  216.8 2.0 collective-permute-done.28
  218.8 2.3 broadcast_select_fusion.1
  221.4 3.0 %collective-permute-done.26 = bf16[4,56,1024]{2,1,0:T(8,128)(2,1)S(1)} collective-permute-done((bf16[4,56,1024]{2,1,0:T(8,128)(2,1)S(1)}, bf16[4,56,1024]{2,1,0:T(8,128)(2,1)S(1)}, u32[]{:S(2)}, u32[]{:S(2)}) %collective-permute-start.26) | collective-permute-done | bytes 458784 | tf_op jit(solution)/shard_map/ppermute | solution.py:26
  225.7 4.0 %multiply_convert_fusion = bf16[896,896]{1,0:T(8,128)(2,1)S(1)} fusion(bf16[896,2048]{1,0:T(8,128)(2,1)S(1)} %bitcast.101, bf16[896,2048]{1,0:T(8,128)(2,1)S(1)} %bitcast.100), kind=kOutput, calls=%fused_computation.2 | convolution fusion | flops 3289939968 | bytes 8945664 | tf_op jit(solution)/shard_map/dot_general | solution.py:255
  231.8 23.6 %all_to_all.5 = bf16[4,224,896]{2,1,0:T(8,128)(2,1)S(1)} all-to-all(bf16[4,224,896]{2,1,0:T(8,128)(2,1)S(1)} %bitcast.94), channel_id=1, replica_groups=mesh['y'=4,'zh'=2,'x'=4,'a'=2,'b'=2,'c'=2] {'y'}, dimensions={0} | all-to-all | bytes 3211264 | tf_op jit(solution)/shard_map/all_to_all | solution.py:261
  255.6 2.1 maximum_convert_fusion
  (118 shorter events, 33.0 us)
Async XLA Ops:
  6.5 208.1 %all-gather.2.cloned.1.call-start = ((), (), s32[]{:S(2)}) async-start(), calls=%async_computation.1 | async-start | bytes 2064384 | tf_op jit(solution)/shard_map/all_gather | solution.py:246
  7.5 14.2 %collective-permute-start.2 = (bf16[64,1024]{1,0:T(8,128)(2,1)S(1)}, bf16[64,1024]{1,0:T(8,128)(2,1)S(1)}, u32[]{:S(2)}, u32[]{:S(2)}) collective-permute-start(bf16[64,1024]{1,0:T(8,128)(2,1)S(1)} %get-tuple-element.91), channel_id=1, source_target_pairs={{0,34},{2,32},{32,2},{34,0},{1,35},{3,33},{33,3},{35,1},{4,38},{6,... | collective-permute-start | bytes 393224 | tf_op jit(solution)/shard_map/ppermute | solution.py:26
  7.7 14.1 %collective-permute-start = (bf16[64,1024]{1,0:T(8,128)(2,1)S(1)}, bf16[64,1024]{1,0:T(8,128)(2,1)S(1)}, u32[]{:S(2)}, u32[]{:S(2)}) collective-permute-start(bf16[64,1024]{1,0:T(8,128)(2,1)S(1)} %get-tuple-element.91), channel_id=1, source_target_pairs={{0,2},{2,0},{1,3},{3,1},{4,6},{6,4},{5,7},{7,5},{8,10},{10,8},{9,1... | collective-permute-start | bytes 393224 | tf_op jit(solution)/shard_map/ppermute | solution.py:26
  9.6 12.1 %collective-permute-start.1 = (bf16[64,1024]{1,0:T(8,128)(2,1)S(1)}, bf16[64,1024]{1,0:T(8,128)(2,1)S(1)}, u32[]{:S(2)}, u32[]{:S(2)}) collective-permute-start(bf16[64,1024]{1,0:T(8,128)(2,1)S(1)} %get-tuple-element.92), channel_id=1, source_target_pairs={{0,32},{32,0},{1,33},{33,1},{2,34},{34,2},{3,35},{35,3},{4,36},{36... | collective-permute-start | bytes 393224 | tf_op jit(solution)/shard_map/ppermute | solution.py:26
  22.0 9.7 %collective-permute-start.3 = (bf16[128,2048]{1,0:T(8,128)(2,1)S(1)}, bf16[128,2048]{1,0:T(8,128)(2,1)S(1)}, u32[]{:S(2)}, u32[]{:S(2)}) collective-permute-start(bf16[128,2048]{1,0:T(8,128)(2,1)S(1)} %get-tuple-element.84), channel_id=1, source_target_pairs={{0,8},{1,65},{8,0},{9,73},{16,24},{17,81},{24,16},{25,89},{64,72},... | collective-permute-start | bytes 1572872 | tf_op jit(solution)/shard_map/ppermute | solution.py:26
  23.6 16.0 %collective-permute-start.4 = (bf16[128,2048]{1,0:T(8,128)(2,1)S(1)}, bf16[128,2048]{1,0:T(8,128)(2,1)S(1)}, u32[]{:S(2)}, u32[]{:S(2)}) collective-permute-start(bf16[128,2048]{1,0:T(8,128)(2,1)S(1)} %get-tuple-element.84), channel_id=1, source_target_pairs={{0,24},{1,193},{8,16},{9,201},{16,8},{17,209},{24,0},{25,217},{64,... | collective-permute-start | bytes 1572872 | tf_op jit(solution)/shard_map/ppermute | solution.py:26
  25.7 13.9 %collective-permute-start.5 = (bf16[128,2048]{1,0:T(8,128)(2,1)S(1)}, bf16[128,2048]{1,0:T(8,128)(2,1)S(1)}, u32[]{:S(2)}, u32[]{:S(2)}) collective-permute-start(bf16[128,2048]{1,0:T(8,128)(2,1)S(1)} %get-tuple-element.84), channel_id=1, source_target_pairs={{0,16},{1,129},{8,24},{9,137},{16,0},{17,145},{24,8},{25,153},{64,... | collective-permute-start | bytes 1572872 | tf_op jit(solution)/shard_map/ppermute | solution.py:26
  26.9 20.1 %collective-permute-start.6 = (bf16[896,384]{1,0:T(8,128)(2,1)S(1)}, bf16[896,384]{1,0:T(8,128)(2,1)S(1)}, u32[]{:S(2)}, u32[]{:S(2)}) collective-permute-start(bf16[896,384]{1,0:T(8,128)(2,1)S(1)} %slice.147), channel_id=1, source_target_pairs={{0,2},{2,0},{1,3},{3,1},{4,6},{6,4},{5,7},{7,5},{8,10},{10,8},{9,1... | collective-permute-start | bytes 2064392 | tf_op jit(solution)/shard_map/ppermute | solution.py:26
  39.9 36.9 %copy-start.7 = (bf16[4,128,2048]{2,1,0:T(8,128)(2,1)}, bf16[4,128,2048]{2,1,0:T(8,128)(2,1)S(1)}, u32[]{:S(2)}) copy-start(bf16[4,128,2048]{2,1,0:T(8,128)(2,1)S(1)} %pad_maximum_fusion.2.refs_3_) | copy-start | bytes 6291460
  47.0 32.7 %copy-start.1 = (bf16[896,384]{1,0:T(8,128)(2,1)}, bf16[896,384]{1,0:T(8,128)(2,1)S(1)}, u32[]{:S(2)}) copy-start(bf16[896,384]{1,0:T(8,128)(2,1)S(1)} %collective-permute-done.6.refs_1_) | copy-start | bytes 2064388
  47.0 29.7 %collective-permute-start.7 = (bf16[4,128,2048]{2,1,0:T(8,128)(2,1)S(1)}, bf16[4,128,2048]{2,1,0:T(8,128)(2,1)S(1)}, u32[]{:S(2)}, u32[]{:S(2)}) collective-permute-start(bf16[4,128,2048]{2,1,0:T(8,128)(2,1)S(1)} %pad_maximum_fusion.2.refs_3_), channel_id=1, source_target_pairs={{0,64},{1,9},{8,72},{9,1},{16,80},{17,25},{24,88},{25,17},{64,0},{... | collective-permute-start | bytes 6291464 | tf_op jit(solution)/shard_map/ppermute | solution.py:26
  47.9 28.8 %collective-permute-start.8 = (bf16[4,128,2048]{2,1,0:T(8,128)(2,1)S(1)}, bf16[4,128,2048]{2,1,0:T(8,128)(2,1)S(1)}, u32[]{:S(2)}, u32[]{:S(2)}) collective-permute-start(bf16[4,128,2048]{2,1,0:T(8,128)(2,1)S(1)} %pad_maximum_fusion.2.refs_3_), channel_id=1, source_target_pairs={{0,192},{1,25},{8,200},{9,17},{16,208},{17,9},{24,216},{25,1},{64,... | collective-permute-start | bytes 6291464 | tf_op jit(solution)/shard_map/ppermute | solution.py:26
  50.2 26.5 %collective-permute-start.9 = (bf16[896,640]{1,0:T(8,128)(2,1)S(1)}, bf16[896,640]{1,0:T(8,128)(2,1)S(1)}, u32[]{:S(2)}, u32[]{:S(2)}) collective-permute-start(bf16[896,640]{1,0:T(8,128)(2,1)S(1)} %slice.148), channel_id=1, source_target_pairs={{0,2},{2,0},{1,3},{3,1},{4,6},{6,4},{5,7},{7,5},{8,10},{10,8},{9,1... | collective-permute-start | bytes 3440648 | tf_op jit(solution)/shard_map/ppermute | solution.py:26
  76.8 16.1 %collective-permute-start.10 = (bf16[2,128,2048]{2,1,0:T(8,128)(2,1)S(1)}, bf16[2,128,2048]{2,1,0:T(8,128)(2,1)S(1)}, u32[]{:S(2)}, u32[]{:S(2)}) collective-permute-start(bf16[2,128,2048]{2,1,0:T(8,128)(2,1)S(1)} %slice.114), channel_id=1, source_target_pairs={{0,192},{1,25},{8,200},{9,17},{16,208},{17,9},{24,216},{25,1},{64,... | collective-permute-start | bytes 3145736 | tf_op jit(solution)/shard_map/ppermute | solution.py:26
  78.6 15.3 %collective-permute-start.11 = (bf16[2,128,2048]{2,1,0:T(8,128)(2,1)S(1)}, bf16[2,128,2048]{2,1,0:T(8,128)(2,1)S(1)}, u32[]{:S(2)}, u32[]{:S(2)}) collective-permute-start(bf16[2,128,2048]{2,1,0:T(8,128)(2,1)S(1)} %slice.115), channel_id=1, source_target_pairs={{0,64},{1,9},{8,72},{9,1},{16,80},{17,25},{24,88},{25,17},{64,0},{... | collective-permute-start | bytes 3145736 | tf_op jit(solution)/shard_map/ppermute | solution.py:26
  94.9 2.8 %collective-permute-start.12 = (bf16[9,2,224,128]{3,2,1,0:T(8,128)(2,1)}, bf16[9,2,224,128]{3,2,1,0:T(8,128)(2,1)S(1)}, u32[]{:S(2)}, u32[]{:S(2)}) collective-permute-start(bf16[9,2,224,128]{3,2,1,0:T(8,128)(2,1)} %get-tuple-element.43), channel_id=1, source_target_pairs={{0,1},{1,0},{2,3},{3,2},{4,5},{5,4},{6,7},{7,6},{8,9},{9,8},{10,11... | collective-permute-start | bytes 3096584 | tf_op jit(solution)/shard_map/ppermute | solution.py:26
  100.0 14.8 %collective-permute-start.13 = (bf16[9,2,56,128]{3,2,1,0:T(8,128)(2,1)S(1)}, bf16[9,2,56,128]{3,2,1,0:T(8,128)(2,1)S(1)}, u32[]{:S(2)}, u32[]{:S(2)}) collective-permute-start(bf16[9,2,56,128]{3,2,1,0:T(8,128)(2,1)S(1)} %get-tuple-element.88), channel_id=1, source_target_pairs={{0,4},{4,0},{1,5},{5,1},{2,6},{6,2},{3,7},{7,3},{8,12},{12,8},{9,1... | collective-permute-start | bytes 774152 | tf_op jit(solution)/shard_map/ppermute | solution.py:26
  114.8 2.3 collective-permute-start.14
  114.9 13.7 %collective-permute-start.15 = (bf16[9,2,56,128]{3,2,1,0:T(8,128)(2,1)S(1)}, bf16[9,2,56,128]{3,2,1,0:T(8,128)(2,1)S(1)}, u32[]{:S(2)}, u32[]{:S(2)}) collective-permute-start(bf16[9,2,56,128]{3,2,1,0:T(8,128)(2,1)S(1)} %get-tuple-element.87), channel_id=1, source_target_pairs={{0,4},{4,0},{1,5},{5,1},{2,6},{6,2},{3,7},{7,3},{8,12},{12,8},{9,1... | collective-permute-start | bytes 774152 | tf_op jit(solution)/shard_map/ppermute | solution.py:26
  128.7 12.2 %collective-permute-start.16 = (bf16[7,2,56,128]{3,2,1,0:T(8,128)(2,1)S(1)}, bf16[7,2,56,128]{3,2,1,0:T(8,128)(2,1)S(1)}, u32[]{:S(2)}, u32[]{:S(2)}) collective-permute-start(bf16[7,2,56,128]{3,2,1,0:T(8,128)(2,1)S(1)} %get-tuple-element.90), channel_id=1, source_target_pairs={{0,4},{4,0},{1,5},{5,1},{2,6},{6,2},{3,7},{7,3},{8,12},{12,8},{9,1... | collective-permute-start | bytes 602120 | tf_op jit(solution)/shard_map/ppermute | solution.py:26
  141.9 13.3 %collective-permute-start.25 = (bf16[56,2048]{1,0:T(8,128)(2,1)S(1)}, bf16[56,2048]{1,0:T(8,128)(2,1)S(1)}, u32[]{:S(2)}, u32[]{:S(2)}) collective-permute-start(bf16[56,2048]{1,0:T(8,128)(2,1)S(1)} %shard_map.48), channel_id=1, source_target_pairs={{2,0},{3,1},{6,4},{7,5},{10,8},{11,9},{14,12},{15,13},{18,16},{19,... | collective-permute-start | bytes 688136 | tf_op jit(solution)/shard_map/ppermute | solution.py:26
  143.2 11.0 %collective-permute-start.18 = (bf16[7,2,56,128]{3,2,1,0:T(8,128)(2,1)S(1)}, bf16[7,2,56,128]{3,2,1,0:T(8,128)(2,1)S(1)}, u32[]{:S(2)}, u32[]{:S(2)}) collective-permute-start(bf16[7,2,56,128]{3,2,1,0:T(8,128)(2,1)S(1)} %get-tuple-element.89), channel_id=1, source_target_pairs={{0,4},{4,0},{1,5},{5,1},{2,6},{6,2},{3,7},{7,3},{8,12},{12,8},{9,1... | collective-permute-start | bytes 602120 | tf_op jit(solution)/shard_map/ppermute | solution.py:26
  156.0 2.0 collective-permute-start.19
  156.6 21.8 %collective-permute-start.17 = (bf16[56,2048]{1,0:T(8,128)(2,1)S(1)}, bf16[56,2048]{1,0:T(8,128)(2,1)S(1)}, u32[]{:S(2)}, u32[]{:S(2)}) collective-permute-start(bf16[56,2048]{1,0:T(8,128)(2,1)S(1)} %shard_map.48), channel_id=1, source_target_pairs={{0,0},{4,16},{8,2},{12,18},{16,4},{20,20},{24,6},{28,22},{1,1},{5,... | collective-permute-start | bytes 688136 | tf_op jit(solution)/shard_map/ppermute | solution.py:26
  178.5 13.0 %collective-permute-start.20 = (bf16[56,2048]{1,0:T(8,128)(2,1)S(1)}, bf16[56,2048]{1,0:T(8,128)(2,1)S(1)}, u32[]{:S(2)}, u32[]{:S(2)}) collective-permute-start(bf16[56,2048]{1,0:T(8,128)(2,1)S(1)} %broadcast_select_fusion.7), channel_id=1, source_target_pairs={{0,8},{1,65},{8,0},{9,73},{16,24},{17,81},{24,16},{25,89},{64,72},... | collective-permute-start | bytes 688136 | tf_op jit(solution)/shard_map/ppermute | solution.py:26
  178.6 18.4 %collective-permute-start.21 = (bf16[56,2048]{1,0:T(8,128)(2,1)S(1)}, bf16[56,2048]{1,0:T(8,128)(2,1)S(1)}, u32[]{:S(2)}, u32[]{:S(2)}) collective-permute-start(bf16[56,2048]{1,0:T(8,128)(2,1)S(1)} %broadcast_select_fusion.7), channel_id=1, source_target_pairs={{0,24},{1,193},{8,16},{9,201},{16,8},{17,209},{24,0},{25,217},{64,... | collective-permute-start | bytes 688136 | tf_op jit(solution)/shard_map/ppermute | solution.py:26
  191.5 8.2 %collective-permute-start.22 = (bf16[56,2048]{1,0:T(8,128)(2,1)S(1)}, bf16[56,2048]{1,0:T(8,128)(2,1)S(1)}, u32[]{:S(2)}, u32[]{:S(2)}) collective-permute-start(bf16[56,2048]{1,0:T(8,128)(2,1)S(1)} %broadcast_select_fusion.7), channel_id=1, source_target_pairs={{0,16},{1,129},{8,24},{9,137},{16,0},{17,145},{24,8},{25,153},{64,... | collective-permute-start | bytes 688136 | tf_op jit(solution)/shard_map/ppermute | solution.py:26
  199.9 13.5 %collective-permute-start.23 = (bf16[4,56,2048]{2,1,0:T(8,128)(2,1)S(1)}, bf16[4,56,2048]{2,1,0:T(8,128)(2,1)S(1)}, u32[]{:S(2)}, u32[]{:S(2)}) collective-permute-start(bf16[4,56,2048]{2,1,0:T(8,128)(2,1)S(1)} %pad_maximum_fusion.5), channel_id=1, source_target_pairs={{0,64},{1,9},{8,72},{9,1},{16,80},{17,25},{24,88},{25,17},{64,0},{... | collective-permute-start | bytes 2752520 | tf_op jit(solution)/shard_map/ppermute | solution.py:26
  200.0 14.7 %collective-permute-start.24 = (bf16[4,56,2048]{2,1,0:T(8,128)(2,1)S(1)}, bf16[4,56,2048]{2,1,0:T(8,128)(2,1)S(1)}, u32[]{:S(2)}, u32[]{:S(2)}) collective-permute-start(bf16[4,56,2048]{2,1,0:T(8,128)(2,1)S(1)} %pad_maximum_fusion.5), channel_id=1, source_target_pairs={{0,192},{1,25},{8,200},{9,17},{16,208},{17,9},{24,216},{25,1},{64,... | collective-permute-start | bytes 2752520 | tf_op jit(solution)/shard_map/ppermute | solution.py:26
  214.6 4.1 %collective-permute-start.28 = (bf16[448,2048]{1,0:T(8,128)(2,1)}, bf16[448,2048]{1,0:T(8,128)(2,1)}, u32[]{:S(2)}, u32[]{:S(2)}) collective-permute-start(bf16[448,2048]{1,0:T(8,128)(2,1)} %all-gather.2.cloned.1.call-done), channel_id=1, source_target_pairs={{0,1},{1,0},{2,3},{3,2},{4,5},{5,4},{6,7},{7,6},{8,9},{9,8},{10,11... | collective-permute-start | bytes 5505032 | tf_op jit(solution)/shard_map/ppermute | solution.py:26
  214.7 9.8 %collective-permute-start.26 = (bf16[4,56,1024]{2,1,0:T(8,128)(2,1)S(1)}, bf16[4,56,1024]{2,1,0:T(8,128)(2,1)S(1)}, u32[]{:S(2)}, u32[]{:S(2)}) collective-permute-start(bf16[4,56,1024]{2,1,0:T(8,128)(2,1)S(1)} %slice.136), channel_id=1, source_target_pairs={{0,192},{1,25},{8,200},{9,17},{16,208},{17,9},{24,216},{25,1},{64,... | collective-permute-start | bytes 1376264 | tf_op jit(solution)/shard_map/ppermute | solution.py:26
  216.6 8.6 %collective-permute-start.27 = (bf16[4,56,1024]{2,1,0:T(8,128)(2,1)S(1)}, bf16[4,56,1024]{2,1,0:T(8,128)(2,1)S(1)}, u32[]{:S(2)}, u32[]{:S(2)}) collective-permute-start(bf16[4,56,1024]{2,1,0:T(8,128)(2,1)S(1)} %slice.137), channel_id=1, source_target_pairs={{0,64},{1,9},{8,72},{9,1},{16,80},{17,25},{24,88},{25,17},{64,0},{... | collective-permute-start | bytes 1376264 | tf_op jit(solution)/shard_map/ppermute | solution.py:26
  (10 other events, 33.0 us)
Sparse Core Ops, SparseCore 0:
  156.1 38.5 all-gather.1
where the time goes:
time: 265 us; the launch traced here: 264 us
  waiting for transfers between devices  134 us (51%)
  starting transfers between devices  46.2 us (17%)
  blocking collectives  23.6 us (9%)
  Pallas kernels  18.2 us (7%)
  other arithmetic  15.8 us (6%)
  between operations  14 us (5%)
  local copies, waits for them, and re-layouts  9 us (3%)
  matrix products  3.99 us (2%)
    ppermute x29, waiting for transfers between devices, move(): return lax.ppermute(value, axes, pairs)  134 us
    ppermute x29, starting transfers between devices, move(): return lax.ppermute(value, axes, pairs)  46.2 us
    all_to_all x1, blocking collectives, local(): scores = lax.all_to_all(scores, 'y', 0, 0, tiled=True)  23.6 us
    pallas_call x4, Pallas kernels, called(): pl.pallas_call(kernel, out_shape=out_shape, in_specs=[pl.BlockSpec(memory...  18.2 us
  transfers between devices with their start and end apart: 30, of which 19 were waited for; matrix products, arithmetic and copies ran while one was open for 4% of the time, Pallas kernels for 7%

commit v1 on v0

--- a/solution.py
+++ b/solution.py
@@ -64,7 +64,7 @@
     return value.reshape(shape)
 
 
-def product_kernel(ranges, tiles, count, *refs):
+def product_kernel(ranges, tiles, turned, count, *refs):
     weights, inputs = refs[:count], refs[count : count + len(ranges)]
     kept_ref, sent_ref, held_weights, held, arrived = refs[count + len(ranges) :]
     width = inputs[0].shape[1]
@@ -94,7 +94,7 @@
         for i in range(blocks):
             block = sums[:, i * width : (i + 1) * width].reshape(2, *kept_ref.shape[1:])
             kept_ref[done + i] = block[0]
-            sent_ref[done + i] = block[1].astype(sent_ref.dtype)
+            sent_ref[turned[done + i]] = block[1].astype(sent_ref.dtype)
         done += blocks
 
 
@@ -112,12 +112,13 @@
     )(*scalars, *arrays)
 
 
-def products(weights, inputs, ranges, tiles):
-    units, count = weights[0].shape[0], sum(blocks for _, blocks in ranges)
+def products(weights, inputs, ranges, tiles, blocks):
+    turned = [blocks.index(place[::-1]) for place in blocks]
+    units, count = weights[0].shape[0], len(blocks)
     _, width, depth = inputs[0].shape
     shape = (count, 2, units // 4, width)
     return called(
-        functools.partial(product_kernel, ranges, tiles, len(weights)),
+        functools.partial(product_kernel, ranges, tiles, turned, len(weights)),
         (jax.ShapeDtypeStruct(shape, jnp.float32), jax.ShapeDtypeStruct(shape, jnp.bfloat16)),
         [
             pltpu.VMEM((units, depth), weights[0].dtype),
@@ -197,9 +198,7 @@
     own, one, three, far_low, far_high, came_two = ring(block, 0, came_two)
     weights = own_weights, came_one, came_two
 
-    def core_sum(kept, sent, order):
-        came = swap(sent, "c")
-        came = jnp.stack([came[i] for i in order])
+    def core_sum(kept, came):
         return (kept + came.astype(jnp.float32)).reshape(-1, 2, 2, quarter, 2 * piece)
 
     def depth_parts(sums):
@@ -207,34 +206,40 @@
         kept = lax.dynamic_index_in_dim(sums, a, 2, keepdims=False)
         return [kept[:, :, :eighth], kept[:, :, eighth:]], [sent[:, :, :eighth], sent[:, :, eighth:]]
 
-    early_blocks = [(i, j) for i in range(3) for j in range(3)]
-    late_blocks = [(i, 3) for i in range(3)] + [(3, j) for j in range(4)]
-    turned = [[blocks.index((j, i)) for i, j in blocks] for blocks in (early_blocks, late_blocks)]
-    early = products(weights, (own, one, three), ((0, 3),) * 3, ((2, 1), (4, 2), (3, 3)))
-    early, far_low, far_high = lax.optimization_barrier((early, far_low, far_high))
-    early = core_sum(*early, turned[0])
-    early, far_low, far_high = lax.optimization_barrier((early, far_low, far_high))
-    early, early_came = depth_parts(early)
-    early_came = [swap(part, "a") for part in early_came]
+    chunks = (
+        [(i, j) for i in range(2) for j in range(2)],
+        [(0, 2), (1, 2), (2, 0), (2, 1), (2, 2)],
+        [(i, 3) for i in range(3)] + [(3, j) for j in range(4)],
+    )
+    kept, sent = products(weights, (own, one), ((0, 2), (0, 2)), ((2, 1), (2, 2)), chunks[0])
+    came = swap(sent, "c")
+    early = products(weights, (own, one, three), ((2, 1), (2, 1), (0, 3)), ((2, 2), (3, 3)), chunks[1])
+    early, came, far_low, far_high = lax.optimization_barrier((early, came, far_low, far_high))
+    first, first_came = depth_parts(core_sum(kept, came))
+    first_came = [swap(part, "a") for part in first_came]
+    came = swap(early[1], "c")
     late = products(
         weights,
         (own, one, three, far_low, far_high),
         ((3, 1),) * 3 + ((0, 2),) * 2,
         ((4, 4), (3, 5)),
-    )
-    late, early_came[0] = lax.optimization_barrier((late, early_came[0]))
-    late = core_sum(*late, turned[1])
-    late, early_came[1] = lax.optimization_barrier((late, early_came[1]))
+        chunks[2],
+    )
+    late, came, first_came = lax.optimization_barrier((late, came, first_came))
+    early, early_came = depth_parts(core_sum(early[0], came))
+    early_came = [swap(part, "a") for part in early_came]
+    late = core_sum(late[0], swap(late[1], "c"))
+    late, early_came = lax.optimization_barrier((late, early_came))
     late, late_came = depth_parts(late)
     late_came = [swap(part, "a") for part in late_came]
 
-    first, second = jnp.where(c == 0, x, y), jnp.where(c == 0, y, x)
+    inner, outer = jnp.where(c == 0, x, y), jnp.where(c == 0, y, x)
     positions = []
-    for i, j in early_blocks + late_blocks:
-        mine, yours = second ^ MASKS[i], first ^ MASKS[j]
+    for i, j in chunks[0] + chunks[1] + chunks[2]:
+        mine, yours = outer ^ MASKS[i], inner ^ MASKS[j]
         positions.append(jnp.where(c == 0, mine * 4 + yours, yours * 4 + mine))
     positions = jnp.stack(positions)
-    norm = [normalized(positions, early[h], early_came[h], late[h], late_came[h]) for h in range(2)]
+    norm = [normalized(positions, first[h], first_came[h], early[h], early_came[h], late[h], late_came[h]) for h in range(2)]
 
     two = move(norm[0], ("b",), lambda b: (0,) if b == 1 else None)
     came = [
@@ -242,20 +247,22 @@
         for h in range(2)
     ]
     one = jnp.where(x % 2 == 0, came[0], came[1])
-    two = jnp.where(is_first, two, norm[1])
+    two, one = lax.optimization_barrier((jnp.where(is_first, two, norm[1]), one))
     two = lax.all_gather(two, ("zh", "a", "b"), axis=0, tiled=True)
-    *one, two = ring(jnp.stack(direct(one)), 2, two)
-    two_core = swap(two, "c")
-    pair = jnp.stack([jnp.where(c == 0, two, two_core), jnp.where(c == 0, two_core, two)])
-    pair = pair.reshape(2, 2, half, tokens).transpose(1, 0, 2, 3).reshape(4 * half, tokens)
-
-    *one, pair = lax.optimization_barrier((*one, pair))
-    one = jnp.stack([*one[:3], jnp.concatenate(one[3:], axis=2)])
-
-    scores = lax.dot_general(
-        one.reshape(4 * half, tokens), pair, (((1,), (1,)), ((), ())), preferred_element_type=jnp.float32
-    )
-    scores = (scores * float(tokens) ** (-0.5)).astype(jnp.bfloat16).reshape(4, 4, eighth, 4 * half)
+    one = ring(jnp.stack(direct(one)), 2)
+    one = jnp.stack([*one[:3], jnp.concatenate(one[3:], axis=2)]).reshape(4 * half, tokens)
+    two, one = lax.optimization_barrier((two, one))
+
+    def score(columns):
+        result = lax.dot_general(one, columns, (((1,), (1,)), ((), ())), preferred_element_type=jnp.float32)
+        return (result * float(tokens) ** (-0.5)).astype(jnp.bfloat16)
+
+    other = swap(two, "c")
+    mine, other = lax.optimization_barrier((score(two), other))
+    other = score(other)
+    low, high = jnp.where(c == 0, mine, other), jnp.where(c == 0, other, mine)
+    scores = jnp.concatenate([low[:, :half], high[:, :half], low[:, half:], high[:, half:]], axis=1)
+    scores = scores.reshape(4, 4, eighth, 4 * half)
     scores = jnp.where(c == 0, scores, scores.swapaxes(0, 1))
     scores = absolute(absolute(scores, y, 0), x, 1).reshape(4, half, 4 * half)
     scores = lax.all_to_all(scores, "y", 0, 0, tiled=True)

time: 265 us -> 258 us (0.974); the launches traced: 264 us -> 254 us
  waiting for transfers between devices: 134 us -> 106 us
  starting transfers between devices: 46.2 us -> 56.5 us
  matrix products: 3.99 us -> 6.95 us
    ppermute x29 -> x32, waiting for transfers between devices: 134 us -> 106 us  [move(): return lax.ppermute(value, axes, pairs)]
    ppermute x29 -> x32, starting transfers between devices: 46.2 us -> 56.5 us  [move(): return lax.ppermute(value, axes, pairs)]
    dot_general x1 -> x2, matrix products: 3.99 us -> 6.95 us  [score(): lax.dot_general(one, columns, (((1,), (1,)), ((), ())), preferred_element...]
    pallas_call x4 -> x5, Pallas kernels: 18.2 us -> 20.8 us  [called(): pl.pallas_call(kernel, out_shape=out_shape, in_specs=[pl.BlockSpec(memory...]
  transfers between devices with their start and end apart: 30 -> 33, of which waited for: 19 -> 18; matrix products, arithmetic and copies ran while one was open for 4% -> 7% of each run, Pallas kernels for 7% -> 8%
where the time goes in v1:
time: 258 us; the launch traced here: 254 us
  waiting for transfers between devices  106 us (41%)
  starting transfers between devices  56.5 us (22%)
  blocking collectives  24.8 us (10%)
  Pallas kernels  20.8 us (8%)
  other arithmetic  14.3 us (6%)
  between operations  14 us (5%)
  local copies, waits for them, and re-layouts  9.96 us (4%)
  matrix products  6.95 us (3%)
    ppermute x32, waiting for transfers between devices, move(): return lax.ppermute(value, axes, pairs)  106 us
    ppermute x32, starting transfers between devices, move(): return lax.ppermute(value, axes, pairs)  56.5 us
    all_to_all x1, blocking collectives, local(): scores = lax.all_to_all(scores, 'y', 0, 0, tiled=True)  24.8 us
    pallas_call x5, Pallas kernels, called(): pl.pallas_call(kernel, out_shape=out_shape, in_specs=[pl.BlockSpec(memory...  20.8 us
    dot_general x2, matrix products, score(): lax.dot_general(one, columns, (((1,), (1,)), ((), ())), preferred_element...  6.95 us
  transfers between devices with their start and end apart: 33, of which 18 were waited for; matrix products, arithmetic and copies ran while one was open for 7% of the time, Pallas kernels for 8%

profile of v1, /device:TPU:224, one launch (start us, length us, event | category | flops | bytes accessed | tf_op | source)
XLA Modules:
  0.0 253.8 jit_solution(15050807419041165339)
XLA Ops:
  9.6 4.5 %collective-permute-start.1 = (bf16[64,1024]{1,0:T(8,128)(2,1)S(1)}, bf16[64,1024]{1,0:T(8,128)(2,1)S(1)}, u32[]{:S(2)}, u32[]{:S(2)}) collective-permute-start(bf16[64,1024]{1,0:T(8,128)(2,1)S(1)} %get-tuple-element.98), channel_id=1, source_target_pairs={{0,32},{32,0},{1,33},{33,1},{2,34},{34,2},{3,35},{35,3},{4,36},{36... | collective-permute-start | bytes 393224 | tf_op jit(solution)/shard_map/ppermute | solution.py:26
  14.1 3.5 %broadcast_select_fusion = (bf16[1024,2,448]{0,2,1:T(8,128)(2,1)}, bf16[1024,2,448]{0,2,1:T(8,128)(2,1)S(1)}) fusion(bf16[1024,2,448]{0,2,1:T(8,128)(2,1)} %param.7, bf16[1024,2,448]{0,2,1:T(8,128)(2,1)} %param.6, pred[]{:T(512)S(6)} %eq.22), kind=kLoop, calls=%fused_computation.10 | loop fusion | flops 1835008 | bytes 7340033 | tf_op jit(solution)/shard_map/jit(_where)/select_n | solution.py:189
  19.3 2.5 collective-permute-done.1
  23.6 2.1 collective-permute-start.4
  26.9 4.8 %collective-permute-start.6 = (bf16[896,384]{1,0:T(8,128)(2,1)S(1)}, bf16[896,384]{1,0:T(8,128)(2,1)S(1)}, u32[]{:S(2)}, u32[]{:S(2)}) collective-permute-start(bf16[896,384]{1,0:T(8,128)(2,1)S(1)} %slice.125), channel_id=1, source_target_pairs={{0,2},{2,0},{1,3},{3,1},{4,6},{6,4},{5,7},{7,5},{8,10},{10,8},{9,1... | collective-permute-start | bytes 2064392 | tf_op jit(solution)/shard_map/ppermute | solution.py:26
  31.7 7.9 %collective-permute-done.4 = bf16[128,2048]{1,0:T(8,128)(2,1)S(1)} collective-permute-done((bf16[128,2048]{1,0:T(8,128)(2,1)S(1)}, bf16[128,2048]{1,0:T(8,128)(2,1)S(1)}, u32[]{:S(2)}, u32[]{:S(2)}) %collective-permute-start.4) | collective-permute-done | bytes 524320 | tf_op jit(solution)/shard_map/ppermute | solution.py:26
  39.9 7.1 %collective-permute-done.6.refs_1_ = bf16[896,384]{1,0:T(8,128)(2,1)S(1)} collective-permute-done((bf16[896,384]{1,0:T(8,128)(2,1)S(1)}, bf16[896,384]{1,0:T(8,128)(2,1)S(1)}, u32[]{:S(2)}, u32[]{:S(2)}) %collective-permute-start.6) | collective-permute-done | bytes 688160 | tf_op jit(solution)/shard_map/ppermute | solution.py:26
  47.9 2.2 collective-permute-start.8
  52.1 24.6 %collective-permute-done.9.refs_2_ = bf16[896,640]{1,0:T(8,128)(2,1)S(1)} collective-permute-done((bf16[896,640]{1,0:T(8,128)(2,1)S(1)}, bf16[896,640]{1,0:T(8,128)(2,1)S(1)}, u32[]{:S(2)}, u32[]{:S(2)}) %collective-permute-start.9) | collective-permute-done | bytes 1146912 | tf_op jit(solution)/shard_map/ppermute | solution.py:26
  81.5 6.1 %shard_map.46 = (f32[4,2,224,128]{3,2,1,0:T(8,128)S(1)}, bf16[4,2,224,128]{3,2,1,0:T(8,128)(2,1)S(1)}) custom-call(bf16[896,1024]{1,0:T(8,128)(2,1)S(1)} %bitcast.90, bf16[896,384]{1,0:T(8,128)(2,1)S(1)} %collective-permute-done.6.refs_1_, bf16[896,640]{1,0:T(8,128)(2,1)S(1)} %collective-permute-done.9.refs_2_, bf16[4,128,2048]{2,1,0:T(8,128)(2,1)} %copy-done.5, ...), custom_call_target="tpu_custom_call" | custom-call | flops 1 | bytes 1 | tf_op jit(solution)/shard_map/pallas_call | solution.py:103
  89.7 5.1 %shard_map.47 = (f32[5,2,224,128]{3,2,1,0:T(8,128)S(1)}, bf16[5,2,224,128]{3,2,1,0:T(8,128)(2,1)S(1)}) custom-call(bf16[896,1024]{1,0:T(8,128)(2,1)S(1)} %bitcast.91, bf16[896,384]{1,0:T(8,128)(2,1)S(1)} %copy-done.2, bf16[896,640]{1,0:T(8,128)(2,1)S(1)} %collective-permute-done.9.refs_2_, bf16[4,128,2048]{2,1,0:T(8,128)(2,1)} %copy-done.5, ...), custom_call_target="tpu_custom_call" | custom-call | flops 1 | bytes 1 | tf_op jit(solution)/shard_map/pallas_call | solution.py:103
  97.6 2.4 collective-permute-start.15
  100.0 7.7 %shard_map.48 = (f32[7,2,224,128]{3,2,1,0:T(8,128)}, bf16[7,2,224,128]{3,2,1,0:T(8,128)(2,1)S(1)}) custom-call(bf16[896,1024]{1,0:T(8,128)(2,1)} %bitcast.92, bf16[896,384]{1,0:T(8,128)(2,1)S(1)} %copy-done.2, bf16[896,640]{1,0:T(8,128)(2,1)S(1)} %collective-permute-done.9.refs_2_, bf16[4,128,2048]{2,1,0:T(8,128)(2,1)} %copy-done.5, ...), custom_call_target="tpu_custom_call" | custom-call | flops 1 | bytes 1 | tf_op jit(solution)/shard_map/pallas_call | solution.py:103
  108.8 2.1 collective-permute-done.15.refs_1_
  111.2 2.9 %collective-permute-start.18 = (bf16[5,2,56,128]{3,2,1,0:T(8,128)(2,1)S(1)}, bf16[5,2,56,128]{3,2,1,0:T(8,128)(2,1)S(1)}, u32[]{:S(2)}, u32[]{:S(2)}) collective-permute-start(bf16[5,2,56,128]{3,2,1,0:T(8,128)(2,1)S(1)} %get-tuple-element.95), channel_id=1, source_target_pairs={{0,4},{4,0},{1,5},{5,1},{2,6},{6,2},{3,7},{7,3},{8,12},{12,8},{9,1... | collective-permute-start | bytes 430088 | tf_op jit(solution)/shard_map/ppermute | solution.py:26
  114.4 8.6 %collective-permute-done.17.refs_3_ = bf16[5,2,56,128]{3,2,1,0:T(8,128)(2,1)S(1)} collective-permute-done((bf16[5,2,56,128]{3,2,1,0:T(8,128)(2,1)S(1)}, bf16[5,2,56,128]{3,2,1,0:T(8,128)(2,1)S(1)}, u32[]{:S(2)}, u32[]{:S(2)}) %collective-permute-start.17) | collective-permute-done | bytes 143392 | tf_op jit(solution)/shard_map/ppermute | solution.py:26
  123.0 3.0 %collective-permute-done.18.refs_3_ = bf16[5,2,56,128]{3,2,1,0:T(8,128)(2,1)S(1)} collective-permute-done((bf16[5,2,56,128]{3,2,1,0:T(8,128)(2,1)S(1)}, bf16[5,2,56,128]{3,2,1,0:T(8,128)(2,1)S(1)}, u32[]{:S(2)}, u32[]{:S(2)}) %collective-permute-start.18) | collective-permute-done | bytes 143392 | tf_op jit(solution)/shard_map/ppermute | solution.py:26
  126.9 12.1 %collective-permute-done.19.refs_5_ = bf16[7,2,56,128]{3,2,1,0:T(8,128)(2,1)S(1)} collective-permute-done((bf16[7,2,56,128]{3,2,1,0:T(8,128)(2,1)S(1)}, bf16[7,2,56,128]{3,2,1,0:T(8,128)(2,1)S(1)}, u32[]{:S(2)}, u32[]{:S(2)}) %collective-permute-start.19) | collective-permute-done | bytes 200736 | tf_op jit(solution)/shard_map/ppermute | solution.py:26
  141.3 2.4 collective-permute-start.21
  145.0 7.2 %collective-permute-done.21.refs_5_ = bf16[7,2,56,128]{3,2,1,0:T(8,128)(2,1)S(1)} collective-permute-done((bf16[7,2,56,128]{3,2,1,0:T(8,128)(2,1)}, bf16[7,2,56,128]{3,2,1,0:T(8,128)(2,1)S(1)}, u32[]{:S(2)}, u32[]{:S(2)}) %collective-permute-start.21) | collective-permute-done | bytes 200736 | tf_op jit(solution)/shard_map/ppermute | solution.py:26
  154.6 2.0 collective-permute-done.22
  156.7 11.6 %collective-permute-start.24 = (bf16[56,2048]{1,0:T(8,128)(2,1)S(1)}, bf16[56,2048]{1,0:T(8,128)(2,1)S(1)}, u32[]{:S(2)}, u32[]{:S(2)}) collective-permute-start(bf16[56,2048]{1,0:T(8,128)(2,1)S(1)} %broadcast_select_fusion.6), channel_id=1, source_target_pairs={{0,8},{1,65},{8,0},{9,73},{16,24},{17,81},{24,16},{25,89},{64,72},... | collective-permute-start | bytes 688136 | tf_op jit(solution)/shard_map/ppermute | solution.py:26
  168.3 6.0 %collective-permute-start.25 = (bf16[56,2048]{1,0:T(8,128)(2,1)S(1)}, bf16[56,2048]{1,0:T(8,128)(2,1)S(1)}, u32[]{:S(2)}, u32[]{:S(2)}) collective-permute-start(bf16[56,2048]{1,0:T(8,128)(2,1)S(1)} %broadcast_select_fusion.6), channel_id=1, source_target_pairs={{0,24},{1,193},{8,16},{9,201},{16,8},{17,209},{24,0},{25,217},{64,... | collective-permute-start | bytes 688136 | tf_op jit(solution)/shard_map/ppermute | solution.py:26
  175.6 4.4 %collective-permute-done.25 = bf16[56,2048]{1,0:T(8,128)(2,1)S(1)} collective-permute-done((bf16[56,2048]{1,0:T(8,128)(2,1)S(1)}, bf16[56,2048]{1,0:T(8,128)(2,1)S(1)}, u32[]{:S(2)}, u32[]{:S(2)}) %collective-permute-start.25) | collective-permute-done | bytes 229408 | tf_op jit(solution)/shard_map/ppermute | solution.py:26
  180.0 2.1 collective-permute-done.26
  184.5 11.2 %collective-permute-done.27 = bf16[4,56,2048]{2,1,0:T(8,128)(2,1)S(1)} collective-permute-done((bf16[4,56,2048]{2,1,0:T(8,128)(2,1)S(1)}, bf16[4,56,2048]{2,1,0:T(8,128)(2,1)S(1)}, u32[]{:S(2)}, u32[]{:S(2)}) %collective-permute-start.27) | collective-permute-done | bytes 917536 | tf_op jit(solution)/shard_map/ppermute | solution.py:26
  198.2 7.3 %collective-permute-done.29 = bf16[4,56,1024]{2,1,0:T(8,128)(2,1)S(1)} collective-permute-done((bf16[4,56,1024]{2,1,0:T(8,128)(2,1)S(1)}, bf16[4,56,1024]{2,1,0:T(8,128)(2,1)S(1)}, u32[]{:S(2)}, u32[]{:S(2)}) %collective-permute-start.29) | collective-permute-done | bytes 458784 | tf_op jit(solution)/shard_map/ppermute | solution.py:26
  206.8 2.1 pad_maximum_fusion
  208.8 4.8 %multiply_convert_fusion.1 = bf16[896,448]{0,1:T(8,128)(2,1)S(1)} fusion(bf16[896,2048]{1,0:T(8,128)(2,1)} %bitcast.104, bf16[448,2048]{1,0:T(8,128)(2,1)} %all-gather.2.cloned.1.call-done), kind=kOutput, calls=%fused_computation.18 | convolution fusion | flops 1644969984 | bytes 6307840 | tf_op jit(solution)/shard_map/dot_general | solution.py:257
  213.7 2.1 multiply_convert_fusion
  220.0 24.8 %all_to_all.5 = bf16[4,224,896]{2,1,0:T(8,128)(2,1)S(1)} all-to-all(bf16[4,224,896]{2,1,0:T(8,128)(2,1)S(1)} %bitcast.101), channel_id=1, replica_groups=mesh['y'=4,'zh'=2,'x'=4,'a'=2,'b'=2,'c'=2] {'y'}, dimensions={0} | all-to-all | bytes 3211264 | tf_op jit(solution)/shard_map/all_to_all | solution.py:268
  244.9 2.1 maximum_convert_fusion
  (118 shorter events, 40.6 us)
Async XLA Ops:
  6.5 202.3 %all-gather.2.cloned.1.call-start = ((), (), s32[]{:S(2)}) async-start(), calls=%async_computation.1 | async-start | bytes 2064384 | tf_op jit(solution)/shard_map/all_gather | solution.py:251
  7.5 14.2 %collective-permute-start.2 = (bf16[64,1024]{1,0:T(8,128)(2,1)S(1)}, bf16[64,1024]{1,0:T(8,128)(2,1)S(1)}, u32[]{:S(2)}, u32[]{:S(2)}) collective-permute-start(bf16[64,1024]{1,0:T(8,128)(2,1)S(1)} %get-tuple-element.97), channel_id=1, source_target_pairs={{0,34},{2,32},{32,2},{34,0},{1,35},{3,33},{33,3},{35,1},{4,38},{6,... | collective-permute-start | bytes 393224 | tf_op jit(solution)/shard_map/ppermute | solution.py:26
  7.7 14.1 %collective-permute-start = (bf16[64,1024]{1,0:T(8,128)(2,1)S(1)}, bf16[64,1024]{1,0:T(8,128)(2,1)S(1)}, u32[]{:S(2)}, u32[]{:S(2)}) collective-permute-start(bf16[64,1024]{1,0:T(8,128)(2,1)S(1)} %get-tuple-element.97), channel_id=1, source_target_pairs={{0,2},{2,0},{1,3},{3,1},{4,6},{6,4},{5,7},{7,5},{8,10},{10,8},{9,1... | collective-permute-start | bytes 393224 | tf_op jit(solution)/shard_map/ppermute | solution.py:26
  9.6 12.1 %collective-permute-start.1 = (bf16[64,1024]{1,0:T(8,128)(2,1)S(1)}, bf16[64,1024]{1,0:T(8,128)(2,1)S(1)}, u32[]{:S(2)}, u32[]{:S(2)}) collective-permute-start(bf16[64,1024]{1,0:T(8,128)(2,1)S(1)} %get-tuple-element.98), channel_id=1, source_target_pairs={{0,32},{32,0},{1,33},{33,1},{2,34},{34,2},{3,35},{35,3},{4,36},{36... | collective-permute-start | bytes 393224 | tf_op jit(solution)/shard_map/ppermute | solution.py:26
  22.0 9.7 %collective-permute-start.3 = (bf16[128,2048]{1,0:T(8,128)(2,1)S(1)}, bf16[128,2048]{1,0:T(8,128)(2,1)S(1)}, u32[]{:S(2)}, u32[]{:S(2)}) collective-permute-start(bf16[128,2048]{1,0:T(8,128)(2,1)S(1)} %get-tuple-element.88), channel_id=1, source_target_pairs={{0,8},{1,65},{8,0},{9,73},{16,24},{17,81},{24,16},{25,89},{64,72},... | collective-permute-start | bytes 1572872 | tf_op jit(solution)/shard_map/ppermute | solution.py:26
  23.6 16.0 %collective-permute-start.4 = (bf16[128,2048]{1,0:T(8,128)(2,1)S(1)}, bf16[128,2048]{1,0:T(8,128)(2,1)S(1)}, u32[]{:S(2)}, u32[]{:S(2)}) collective-permute-start(bf16[128,2048]{1,0:T(8,128)(2,1)S(1)} %get-tuple-element.88), channel_id=1, source_target_pairs={{0,24},{1,193},{8,16},{9,201},{16,8},{17,209},{24,0},{25,217},{64,... | collective-permute-start | bytes 1572872 | tf_op jit(solution)/shard_map/ppermute | solution.py:26
  25.7 13.9 %collective-permute-start.5 = (bf16[128,2048]{1,0:T(8,128)(2,1)S(1)}, bf16[128,2048]{1,0:T(8,128)(2,1)S(1)}, u32[]{:S(2)}, u32[]{:S(2)}) collective-permute-start(bf16[128,2048]{1,0:T(8,128)(2,1)S(1)} %get-tuple-element.88), channel_id=1, source_target_pairs={{0,16},{1,129},{8,24},{9,137},{16,0},{17,145},{24,8},{25,153},{64,... | collective-permute-start | bytes 1572872 | tf_op jit(solution)/shard_map/ppermute | solution.py:26
  26.9 20.1 %collective-permute-start.6 = (bf16[896,384]{1,0:T(8,128)(2,1)S(1)}, bf16[896,384]{1,0:T(8,128)(2,1)S(1)}, u32[]{:S(2)}, u32[]{:S(2)}) collective-permute-start(bf16[896,384]{1,0:T(8,128)(2,1)S(1)} %slice.125), channel_id=1, source_target_pairs={{0,2},{2,0},{1,3},{3,1},{4,6},{6,4},{5,7},{7,5},{8,10},{10,8},{9,1... | collective-permute-start | bytes 2064392 | tf_op jit(solution)/shard_map/ppermute | solution.py:26
  47.0 29.7 %collective-permute-start.7 = (bf16[4,128,2048]{2,1,0:T(8,128)(2,1)S(1)}, bf16[4,128,2048]{2,1,0:T(8,128)(2,1)S(1)}, u32[]{:S(2)}, u32[]{:S(2)}) collective-permute-start(bf16[4,128,2048]{2,1,0:T(8,128)(2,1)S(1)} %pad_maximum_fusion.1.refs_3_), channel_id=1, source_target_pairs={{0,64},{1,9},{8,72},{9,1},{16,80},{17,25},{24,88},{25,17},{64,0},{... | collective-permute-start | bytes 6291464 | tf_op jit(solution)/shard_map/ppermute | solution.py:26
  47.9 28.8 %collective-permute-start.8 = (bf16[4,128,2048]{2,1,0:T(8,128)(2,1)S(1)}, bf16[4,128,2048]{2,1,0:T(8,128)(2,1)S(1)}, u32[]{:S(2)}, u32[]{:S(2)}) collective-permute-start(bf16[4,128,2048]{2,1,0:T(8,128)(2,1)S(1)} %pad_maximum_fusion.1.refs_3_), channel_id=1, source_target_pairs={{0,192},{1,25},{8,200},{9,17},{16,208},{17,9},{24,216},{25,1},{64,... | collective-permute-start | bytes 6291464 | tf_op jit(solution)/shard_map/ppermute | solution.py:26
  50.2 26.5 %collective-permute-start.9 = (bf16[896,640]{1,0:T(8,128)(2,1)S(1)}, bf16[896,640]{1,0:T(8,128)(2,1)S(1)}, u32[]{:S(2)}, u32[]{:S(2)}) collective-permute-start(bf16[896,640]{1,0:T(8,128)(2,1)S(1)} %slice.126), channel_id=1, source_target_pairs={{0,2},{2,0},{1,3},{3,1},{4,6},{6,4},{5,7},{7,5},{8,10},{10,8},{9,1... | collective-permute-start | bytes 3440648 | tf_op jit(solution)/shard_map/ppermute | solution.py:26
  78.0 16.9 %collective-permute-start.11 = (bf16[2,128,2048]{2,1,0:T(8,128)(2,1)}, bf16[2,128,2048]{2,1,0:T(8,128)(2,1)}, u32[]{:S(2)}, u32[]{:S(2)}) collective-permute-start(bf16[2,128,2048]{2,1,0:T(8,128)(2,1)} %slice.96), channel_id=1, source_target_pairs={{0,192},{1,25},{8,200},{9,17},{16,208},{17,9},{24,216},{25,1},{64,... | collective-permute-start | bytes 3145736 | tf_op jit(solution)/shard_map/ppermute | solution.py:26
  80.7 15.1 %collective-permute-start.12 = (bf16[2,128,2048]{2,1,0:T(8,128)(2,1)}, bf16[2,128,2048]{2,1,0:T(8,128)(2,1)}, u32[]{:S(2)}, u32[]{:S(2)}) collective-permute-start(bf16[2,128,2048]{2,1,0:T(8,128)(2,1)} %slice.97), channel_id=1, source_target_pairs={{0,64},{1,9},{8,72},{9,1},{16,80},{17,25},{24,88},{25,17},{64,0},{... | collective-permute-start | bytes 3145736 | tf_op jit(solution)/shard_map/ppermute | solution.py:26
  88.5 6.4 %collective-permute-start.10 = (bf16[4,2,224,128]{3,2,1,0:T(8,128)(2,1)S(1)}, bf16[4,2,224,128]{3,2,1,0:T(8,128)(2,1)}, u32[]{:S(2)}, u32[]{:S(2)}) collective-permute-start(bf16[4,2,224,128]{3,2,1,0:T(8,128)(2,1)S(1)} %get-tuple-element.43), channel_id=1, source_target_pairs={{0,1},{1,0},{2,3},{3,2},{4,5},{5,4},{6,7},{7,6},{8,9},{9,8},{10,11... | collective-permute-start | bytes 1376264 | tf_op jit(solution)/shard_map/ppermute | solution.py:26
  95.8 15.1 %collective-permute-start.13 = (bf16[5,2,224,128]{3,2,1,0:T(8,128)(2,1)S(1)}, bf16[5,2,224,128]{3,2,1,0:T(8,128)(2,1)S(1)}, u32[]{:S(2)}, u32[]{:S(2)}) collective-permute-start(bf16[5,2,224,128]{3,2,1,0:T(8,128)(2,1)S(1)} %get-tuple-element.49), channel_id=1, source_target_pairs={{0,1},{1,0},{2,3},{3,2},{4,5},{5,4},{6,7},{7,6},{8,9},{9,8},{10,11... | collective-permute-start | bytes 1720328 | tf_op jit(solution)/shard_map/ppermute | solution.py:26
  97.0 11.8 %collective-permute-start.14 = (bf16[4,2,56,128]{3,2,1,0:T(8,128)(2,1)S(1)}, bf16[4,2,56,128]{3,2,1,0:T(8,128)(2,1)S(1)}, u32[]{:S(2)}, u32[]{:S(2)}) collective-permute-start(bf16[4,2,56,128]{3,2,1,0:T(8,128)(2,1)S(1)} %get-tuple-element.100), channel_id=1, source_target_pairs={{0,4},{4,0},{1,5},{5,1},{2,6},{6,2},{3,7},{7,3},{8,12},{12,8},{9,1... | collective-permute-start | bytes 344072 | tf_op jit(solution)/shard_map/ppermute | solution.py:26
  97.6 13.3 %collective-permute-start.15 = (bf16[4,2,56,128]{3,2,1,0:T(8,128)(2,1)S(1)}, bf16[4,2,56,128]{3,2,1,0:T(8,128)(2,1)S(1)}, u32[]{:S(2)}, u32[]{:S(2)}) collective-permute-start(bf16[4,2,56,128]{3,2,1,0:T(8,128)(2,1)S(1)} %get-tuple-element.99), channel_id=1, source_target_pairs={{0,4},{4,0},{1,5},{5,1},{2,6},{6,2},{3,7},{7,3},{8,12},{12,8},{9,1... | collective-permute-start | bytes 344072 | tf_op jit(solution)/shard_map/ppermute | solution.py:26
  110.9 3.3 %collective-permute-start.16 = (bf16[7,2,224,128]{3,2,1,0:T(8,128)(2,1)S(1)}, bf16[7,2,224,128]{3,2,1,0:T(8,128)(2,1)S(1)}, u32[]{:S(2)}, u32[]{:S(2)}) collective-permute-start(bf16[7,2,224,128]{3,2,1,0:T(8,128)(2,1)S(1)} %get-tuple-element.54), channel_id=1, source_target_pairs={{0,1},{1,0},{2,3},{3,2},{4,5},{5,4},{6,7},{7,6},{8,9},{9,8},{10,11... | collective-permute-start | bytes 2408456 | tf_op jit(solution)/shard_map/ppermute | solution.py:26
  111.1 11.9 %collective-permute-start.17 = (bf16[5,2,56,128]{3,2,1,0:T(8,128)(2,1)S(1)}, bf16[5,2,56,128]{3,2,1,0:T(8,128)(2,1)S(1)}, u32[]{:S(2)}, u32[]{:S(2)}) collective-permute-start(bf16[5,2,56,128]{3,2,1,0:T(8,128)(2,1)S(1)} %get-tuple-element.96), channel_id=1, source_target_pairs={{0,4},{4,0},{1,5},{5,1},{2,6},{6,2},{3,7},{7,3},{8,12},{12,8},{9,1... | collective-permute-start | bytes 430088 | tf_op jit(solution)/shard_map/ppermute | solution.py:26
  111.2 14.8 %collective-permute-start.18 = (bf16[5,2,56,128]{3,2,1,0:T(8,128)(2,1)S(1)}, bf16[5,2,56,128]{3,2,1,0:T(8,128)(2,1)S(1)}, u32[]{:S(2)}, u32[]{:S(2)}) collective-permute-start(bf16[5,2,56,128]{3,2,1,0:T(8,128)(2,1)S(1)} %get-tuple-element.95), channel_id=1, source_target_pairs={{0,4},{4,0},{1,5},{5,1},{2,6},{6,2},{3,7},{7,3},{8,12},{12,8},{9,1... | collective-permute-start | bytes 430088 | tf_op jit(solution)/shard_map/ppermute | solution.py:26
  126.8 12.2 %collective-permute-start.19 = (bf16[7,2,56,128]{3,2,1,0:T(8,128)(2,1)S(1)}, bf16[7,2,56,128]{3,2,1,0:T(8,128)(2,1)S(1)}, u32[]{:S(2)}, u32[]{:S(2)}) collective-permute-start(bf16[7,2,56,128]{3,2,1,0:T(8,128)(2,1)S(1)} %get-tuple-element.94), channel_id=1, source_target_pairs={{0,4},{4,0},{1,5},{5,1},{2,6},{6,2},{3,7},{7,3},{8,12},{12,8},{9,1... | collective-permute-start | bytes 602120 | tf_op jit(solution)/shard_map/ppermute | solution.py:26
  140.0 13.9 %collective-permute-start.20 = (bf16[56,2048]{1,0:T(8,128)(2,1)S(1)}, bf16[56,2048]{1,0:T(8,128)(2,1)S(1)}, u32[]{:S(2)}, u32[]{:S(2)}) collective-permute-start(bf16[56,2048]{1,0:T(8,128)(2,1)S(1)} %shard_map.49), channel_id=1, source_target_pairs={{2,0},{3,1},{6,4},{7,5},{10,8},{11,9},{14,12},{15,13},{18,16},{19,... | collective-permute-start | bytes 688136 | tf_op jit(solution)/shard_map/ppermute | solution.py:26
  141.3 11.0 %collective-permute-start.21 = (bf16[7,2,56,128]{3,2,1,0:T(8,128)(2,1)}, bf16[7,2,56,128]{3,2,1,0:T(8,128)(2,1)S(1)}, u32[]{:S(2)}, u32[]{:S(2)}) collective-permute-start(bf16[7,2,56,128]{3,2,1,0:T(8,128)(2,1)} %get-tuple-element.93), channel_id=1, source_target_pairs={{0,4},{4,0},{1,5},{5,1},{2,6},{6,2},{3,7},{7,3},{8,12},{12,8},{9,1... | collective-permute-start | bytes 602120 | tf_op jit(solution)/shard_map/ppermute | solution.py:26
  143.7 12.9 %collective-permute-start.22 = (bf16[56,2048]{1,0:T(8,128)(2,1)S(1)}, bf16[56,2048]{1,0:T(8,128)(2,1)S(1)}, u32[]{:S(2)}, u32[]{:S(2)}) collective-permute-start(bf16[56,2048]{1,0:T(8,128)(2,1)S(1)} %shard_map.49), channel_id=1, source_target_pairs={{0,0},{4,16},{8,2},{12,18},{16,4},{20,20},{24,6},{28,22},{1,1},{5,... | collective-permute-start | bytes 688136 | tf_op jit(solution)/shard_map/ppermute | solution.py:26
  156.7 18.9 %collective-permute-start.24 = (bf16[56,2048]{1,0:T(8,128)(2,1)S(1)}, bf16[56,2048]{1,0:T(8,128)(2,1)S(1)}, u32[]{:S(2)}, u32[]{:S(2)}) collective-permute-start(bf16[56,2048]{1,0:T(8,128)(2,1)S(1)} %broadcast_select_fusion.6), channel_id=1, source_target_pairs={{0,8},{1,65},{8,0},{9,73},{16,24},{17,81},{24,16},{25,89},{64,72},... | collective-permute-start | bytes 688136 | tf_op jit(solution)/shard_map/ppermute | solution.py:26
  168.3 11.8 %collective-permute-start.25 = (bf16[56,2048]{1,0:T(8,128)(2,1)S(1)}, bf16[56,2048]{1,0:T(8,128)(2,1)S(1)}, u32[]{:S(2)}, u32[]{:S(2)}) collective-permute-start(bf16[56,2048]{1,0:T(8,128)(2,1)S(1)} %broadcast_select_fusion.6), channel_id=1, source_target_pairs={{0,24},{1,193},{8,16},{9,201},{16,8},{17,209},{24,0},{25,217},{64,... | collective-permute-start | bytes 688136 | tf_op jit(solution)/shard_map/ppermute | solution.py:26
  174.3 7.8 %collective-permute-start.26 = (bf16[56,2048]{1,0:T(8,128)(2,1)S(1)}, bf16[56,2048]{1,0:T(8,128)(2,1)S(1)}, u32[]{:S(2)}, u32[]{:S(2)}) collective-permute-start(bf16[56,2048]{1,0:T(8,128)(2,1)S(1)} %broadcast_select_fusion.6), channel_id=1, source_target_pairs={{0,16},{1,129},{8,24},{9,137},{16,0},{17,145},{24,8},{25,153},{64,... | collective-permute-start | bytes 688136 | tf_op jit(solution)/shard_map/ppermute | solution.py:26
  182.2 13.5 %collective-permute-start.27 = (bf16[4,56,2048]{2,1,0:T(8,128)(2,1)S(1)}, bf16[4,56,2048]{2,1,0:T(8,128)(2,1)S(1)}, u32[]{:S(2)}, u32[]{:S(2)}) collective-permute-start(bf16[4,56,2048]{2,1,0:T(8,128)(2,1)S(1)} %get-tuple-element.78), channel_id=1, source_target_pairs={{0,64},{1,9},{8,72},{9,1},{16,80},{17,25},{24,88},{25,17},{64,0},{... | collective-permute-start | bytes 2752520 | tf_op jit(solution)/shard_map/ppermute | solution.py:26
  183.5 14.6 %collective-permute-start.28 = (bf16[4,56,2048]{2,1,0:T(8,128)(2,1)S(1)}, bf16[4,56,2048]{2,1,0:T(8,128)(2,1)S(1)}, u32[]{:S(2)}, u32[]{:S(2)}) collective-permute-start(bf16[4,56,2048]{2,1,0:T(8,128)(2,1)S(1)} %get-tuple-element.78), channel_id=1, source_target_pairs={{0,192},{1,25},{8,200},{9,17},{16,208},{17,9},{24,216},{25,1},{64,... | collective-permute-start | bytes 2752520 | tf_op jit(solution)/shard_map/ppermute | solution.py:26
  195.8 9.8 %collective-permute-start.29 = (bf16[4,56,1024]{2,1,0:T(8,128)(2,1)S(1)}, bf16[4,56,1024]{2,1,0:T(8,128)(2,1)S(1)}, u32[]{:S(2)}, u32[]{:S(2)}) collective-permute-start(bf16[4,56,1024]{2,1,0:T(8,128)(2,1)S(1)} %slice.139), channel_id=1, source_target_pairs={{0,192},{1,25},{8,200},{9,17},{16,208},{17,9},{24,216},{25,1},{64,... | collective-permute-start | bytes 1376264 | tf_op jit(solution)/shard_map/ppermute | solution.py:26
  198.1 8.6 %collective-permute-start.30 = (bf16[4,56,1024]{2,1,0:T(8,128)(2,1)S(1)}, bf16[4,56,1024]{2,1,0:T(8,128)(2,1)S(1)}, u32[]{:S(2)}, u32[]{:S(2)}) collective-permute-start(bf16[4,56,1024]{2,1,0:T(8,128)(2,1)S(1)} %slice.140), channel_id=1, source_target_pairs={{0,64},{1,9},{8,72},{9,1},{16,80},{17,25},{24,88},{25,17},{64,0},{... | collective-permute-start | bytes 1376264 | tf_op jit(solution)/shard_map/ppermute | solution.py:26
  208.8 4.9 %collective-permute-start.31 = (bf16[448,2048]{1,0:T(8,128)(2,1)}, bf16[448,2048]{1,0:T(8,128)(2,1)S(1)}, u32[]{:S(2)}, u32[]{:S(2)}) collective-permute-start(bf16[448,2048]{1,0:T(8,128)(2,1)} %all-gather.2.cloned.1.call-done), channel_id=1, source_target_pairs={{0,1},{1,0},{2,3},{3,2},{4,5},{5,4},{6,7},{7,6},{8,9},{9,8},{10,11... | collective-permute-start | bytes 5505032 | tf_op jit(solution)/shard_map/ppermute | solution.py:26
  (11 other events, 106.0 us)
Sparse Core Ops, SparseCore 0:
  156.8 50.8 all-gather.1

commit v2 on v1

--- a/solution.py
+++ b/solution.py
@@ -201,10 +201,13 @@
     def core_sum(kept, came):
         return (kept + came.astype(jnp.float32)).reshape(-1, 2, 2, quarter, 2 * piece)
 
+    def halves(value):
+        return [value[:, :, :eighth], value[:, :, eighth:]]
+
     def depth_parts(sums):
         sent = lax.dynamic_index_in_dim(sums, 1 - a, 2, keepdims=False).astype(jnp.bfloat16)
         kept = lax.dynamic_index_in_dim(sums, a, 2, keepdims=False)
-        return [kept[:, :, :eighth], kept[:, :, eighth:]], [sent[:, :, :eighth], sent[:, :, eighth:]]
+        return halves(kept), sent
 
     chunks = (
         [(i, j) for i in range(2) for j in range(2)],
@@ -216,7 +219,7 @@
     early = products(weights, (own, one, three), ((2, 1), (2, 1), (0, 3)), ((2, 2), (3, 3)), chunks[1])
     early, came, far_low, far_high = lax.optimization_barrier((early, came, far_low, far_high))
     first, first_came = depth_parts(core_sum(kept, came))
-    first_came = [swap(part, "a") for part in first_came]
+    first_came = swap(first_came, "a")
     came = swap(early[1], "c")
     late = products(
         weights,
@@ -227,11 +230,12 @@
     )
     late, came, first_came = lax.optimization_barrier((late, came, first_came))
     early, early_came = depth_parts(core_sum(early[0], came))
-    early_came = [swap(part, "a") for part in early_came]
+    early_came = swap(early_came, "a")
     late = core_sum(late[0], swap(late[1], "c"))
     late, early_came = lax.optimization_barrier((late, early_came))
     late, late_came = depth_parts(late)
-    late_came = [swap(part, "a") for part in late_came]
+    late_came = [swap(part, "a") for part in halves(late_came)]
+    first_came, early_came = halves(first_came), halves(early_came)
 
     inner, outer = jnp.where(c == 0, x, y), jnp.where(c == 0, y, x)
     positions = []

time: 258 us -> 257 us (level)
  waiting for transfers between devices: 106 us -> 112 us
  starting transfers between devices: 56.5 us -> 51.2 us
    ppermute x32 -> x30, starting transfers between devices: 56.5 us -> 51.2 us  [move(): return lax.ppermute(value, axes, pairs)]
    ppermute x32 -> x30, waiting for transfers between devices: 106 us -> 112 us  [move(): return lax.ppermute(value, axes, pairs)]
  transfers between devices with their start and end apart: 33 -> 31, of which waited for: 18 -> 17; matrix products, arithmetic and copies ran while one was open for 7% -> 7% of each run, Pallas kernels for 8% -> 8%
where the time goes in v2:
time: 257 us; the launch traced here: 253 us
  waiting for transfers between devices  112 us (44%)
  starting transfers between devices  51.2 us (20%)
  blocking collectives  25.1 us (10%)
  Pallas kernels  20.8 us (8%)
  other arithmetic  14.4 us (6%)
  between operations  14 us (5%)
  local copies, waits for them, and re-layouts  9.32 us (4%)
  matrix products  6.95 us (3%)
    ppermute x30, waiting for transfers between devices, move(): return lax.ppermute(value, axes, pairs)  112 us
    ppermute x30, starting transfers between devices, move(): return lax.ppermute(value, axes, pairs)  51.2 us
    all_to_all x1, blocking collectives, local(): scores = lax.all_to_all(scores, 'y', 0, 0, tiled=True)  25.1 us
    pallas_call x5, Pallas kernels, called(): pl.pallas_call(kernel, out_shape=out_shape, in_specs=[pl.BlockSpec(memory...  20.8 us
    dot_general x2, matrix products, score(): lax.dot_general(one, columns, (((1,), (1,)), ((), ())), preferred_element...  6.95 us
  transfers between devices with their start and end apart: 31, of which 17 were waited for; matrix products, arithmetic and copies ran while one was open for 7% of the time, Pallas kernels for 8%

profile of v2, /device:TPU:224, one launch (start us, length us, event | category | flops | bytes accessed | tf_op | source)
XLA Modules:
  0.0 253.2 jit_solution(7519737960724959953)
XLA Ops:
  7.7 1.9 collective-permute-start
  9.6 4.5 %collective-permute-start.1 = (bf16[64,1024]{1,0:T(8,128)(2,1)S(1)}, bf16[64,1024]{1,0:T(8,128)(2,1)S(1)}, u32[]{:S(2)}, u32[]{:S(2)}) collective-permute-start(bf16[64,1024]{1,0:T(8,128)(2,1)S(1)} %get-tuple-element.94), channel_id=1, source_target_pairs={{0,32},{32,0},{1,33},{33,1},{2,34},{34,2},{3,35},{35,3},{4,36},{36... | collective-permute-start | bytes 393224 | tf_op jit(solution)/shard_map/ppermute | solution.py:26
  14.1 3.5 %broadcast_select_fusion = (bf16[1024,2,448]{0,2,1:T(8,128)(2,1)}, bf16[1024,2,448]{0,2,1:T(8,128)(2,1)S(1)}) fusion(bf16[1024,2,448]{0,2,1:T(8,128)(2,1)} %param.7, bf16[1024,2,448]{0,2,1:T(8,128)(2,1)} %param.6, pred[]{:T(512)S(6)} %eq.22), kind=kLoop, calls=%fused_computation.10 | loop fusion | flops 1835008 | bytes 7340033 | tf_op jit(solution)/shard_map/jit(_where)/select_n | solution.py:189
  19.3 2.5 collective-permute-done.1
  23.6 2.1 collective-permute-start.4
  26.9 4.8 %collective-permute-start.6 = (bf16[896,384]{1,0:T(8,128)(2,1)S(1)}, bf16[896,384]{1,0:T(8,128)(2,1)S(1)}, u32[]{:S(2)}, u32[]{:S(2)}) collective-permute-start(bf16[896,384]{1,0:T(8,128)(2,1)S(1)} %slice.125), channel_id=1, source_target_pairs={{0,2},{2,0},{1,3},{3,1},{4,6},{6,4},{5,7},{7,5},{8,10},{10,8},{9,1... | collective-permute-start | bytes 2064392 | tf_op jit(solution)/shard_map/ppermute | solution.py:26
  31.7 7.9 %collective-permute-done.4 = bf16[128,2048]{1,0:T(8,128)(2,1)S(1)} collective-permute-done((bf16[128,2048]{1,0:T(8,128)(2,1)S(1)}, bf16[128,2048]{1,0:T(8,128)(2,1)S(1)}, u32[]{:S(2)}, u32[]{:S(2)}) %collective-permute-start.4) | collective-permute-done | bytes 524320 | tf_op jit(solution)/shard_map/ppermute | solution.py:26
  39.9 7.1 %collective-permute-done.6.refs_1_ = bf16[896,384]{1,0:T(8,128)(2,1)S(1)} collective-permute-done((bf16[896,384]{1,0:T(8,128)(2,1)S(1)}, bf16[896,384]{1,0:T(8,128)(2,1)S(1)}, u32[]{:S(2)}, u32[]{:S(2)}) %collective-permute-start.6) | collective-permute-done | bytes 688160 | tf_op jit(solution)/shard_map/ppermute | solution.py:26
  47.9 2.2 collective-permute-start.8
  50.2 1.8 collective-permute-start.9
  52.1 24.6 %collective-permute-done.9.refs_2_ = bf16[896,640]{1,0:T(8,128)(2,1)S(1)} collective-permute-done((bf16[896,640]{1,0:T(8,128)(2,1)S(1)}, bf16[896,640]{1,0:T(8,128)(2,1)S(1)}, u32[]{:S(2)}, u32[]{:S(2)}) %collective-permute-start.9) | collective-permute-done | bytes 1146912 | tf_op jit(solution)/shard_map/ppermute | solution.py:26
  81.5 6.1 %shard_map.46 = (f32[4,2,224,128]{3,2,1,0:T(8,128)S(1)}, bf16[4,2,224,128]{3,2,1,0:T(8,128)(2,1)S(1)}) custom-call(bf16[896,1024]{1,0:T(8,128)(2,1)S(1)} %bitcast.90, bf16[896,384]{1,0:T(8,128)(2,1)S(1)} %collective-permute-done.6.refs_1_, bf16[896,640]{1,0:T(8,128)(2,1)S(1)} %collective-permute-done.9.refs_2_, bf16[4,128,2048]{2,1,0:T(8,128)(2,1)} %copy-done.5, ...), custom_call_target="tpu_custom_call" | custom-call | flops 1 | bytes 1 | tf_op jit(solution)/shard_map/pallas_call | solution.py:103
  89.8 5.1 %shard_map.47 = (f32[5,2,224,128]{3,2,1,0:T(8,128)S(1)}, bf16[5,2,224,128]{3,2,1,0:T(8,128)(2,1)S(1)}) custom-call(bf16[896,1024]{1,0:T(8,128)(2,1)S(1)} %bitcast.91, bf16[896,384]{1,0:T(8,128)(2,1)S(1)} %copy-done.2, bf16[896,640]{1,0:T(8,128)(2,1)S(1)} %collective-permute-done.9.refs_2_, bf16[4,128,2048]{2,1,0:T(8,128)(2,1)} %copy-done.5, ...), custom_call_target="tpu_custom_call" | custom-call | flops 1 | bytes 1 | tf_op jit(solution)/shard_map/pallas_call | solution.py:103
  97.6 7.6 %shard_map.48 = (f32[7,2,224,128]{3,2,1,0:T(8,128)}, bf16[7,2,224,128]{3,2,1,0:T(8,128)(2,1)S(1)}) custom-call(bf16[896,1024]{1,0:T(8,128)(2,1)} %bitcast.92, bf16[896,384]{1,0:T(8,128)(2,1)S(1)} %copy-done.2, bf16[896,640]{1,0:T(8,128)(2,1)S(1)} %collective-permute-done.9.refs_2_, bf16[4,128,2048]{2,1,0:T(8,128)(2,1)} %copy-done.5, ...), custom_call_target="tpu_custom_call" | custom-call | flops 1 | bytes 1 | tf_op jit(solution)/shard_map/pallas_call | solution.py:103
  105.3 5.6 %collective-permute-done.14 = bf16[4,2,112,128]{3,2,1,0:T(8,128)(2,1)S(1)} collective-permute-done((bf16[4,2,112,128]{3,2,1,0:T(8,128)(2,1)S(1)}, bf16[4,2,112,128]{3,2,1,0:T(8,128)(2,1)S(1)}, u32[]{:S(2)}, u32[]{:S(2)}) %collective-permute-start.14) | collective-permute-done | bytes 229408 | tf_op jit(solution)/shard_map/ppermute | solution.py:26
  111.3 1.9 collective-permute-done.15
  113.3 12.6 %collective-permute-done.16 = bf16[5,2,112,128]{3,2,1,0:T(8,128)(2,1)S(1)} collective-permute-done((bf16[5,2,112,128]{3,2,1,0:T(8,128)(2,1)S(1)}, bf16[5,2,112,128]{3,2,1,0:T(8,128)(2,1)S(1)}, u32[]{:S(2)}, u32[]{:S(2)}) %collective-permute-start.16) | collective-permute-done | bytes 286752 | tf_op jit(solution)/shard_map/ppermute | solution.py:26
  126.3 12.1 %collective-permute-done.17.refs_5_ = bf16[7,2,56,128]{3,2,1,0:T(8,128)(2,1)S(1)} collective-permute-done((bf16[7,2,56,128]{3,2,1,0:T(8,128)(2,1)S(1)}, bf16[7,2,56,128]{3,2,1,0:T(8,128)(2,1)S(1)}, u32[]{:S(2)}, u32[]{:S(2)}) %collective-permute-start.17) | collective-permute-done | bytes 200736 | tf_op jit(solution)/shard_map/ppermute | solution.py:26
  140.7 2.4 collective-permute-start.19
  144.5 7.0 %collective-permute-done.19.refs_5_ = bf16[7,2,56,128]{3,2,1,0:T(8,128)(2,1)S(1)} collective-permute-done((bf16[7,2,56,128]{3,2,1,0:T(8,128)(2,1)S(1)}, bf16[7,2,56,128]{3,2,1,0:T(8,128)(2,1)S(1)}, u32[]{:S(2)}, u32[]{:S(2)}) %collective-permute-start.19) | collective-permute-done | bytes 200736 | tf_op jit(solution)/shard_map/ppermute | solution.py:26
  153.9 2.3 collective-permute-done.20
  156.2 11.1 %collective-permute-start.22 = (bf16[56,2048]{1,0:T(8,128)(2,1)S(1)}, bf16[56,2048]{1,0:T(8,128)(2,1)S(1)}, u32[]{:S(2)}, u32[]{:S(2)}) collective-permute-start(bf16[56,2048]{1,0:T(8,128)(2,1)S(1)} %broadcast_select_fusion.6), channel_id=1, source_target_pairs={{0,8},{1,65},{8,0},{9,73},{16,24},{17,81},{24,16},{25,89},{64,72},... | collective-permute-start | bytes 688136 | tf_op jit(solution)/shard_map/ppermute | solution.py:26
  167.3 6.1 %collective-permute-start.23 = (bf16[56,2048]{1,0:T(8,128)(2,1)S(1)}, bf16[56,2048]{1,0:T(8,128)(2,1)S(1)}, u32[]{:S(2)}, u32[]{:S(2)}) collective-permute-start(bf16[56,2048]{1,0:T(8,128)(2,1)S(1)} %broadcast_select_fusion.6), channel_id=1, source_target_pairs={{0,24},{1,193},{8,16},{9,201},{16,8},{17,209},{24,0},{25,217},{64,... | collective-permute-start | bytes 688136 | tf_op jit(solution)/shard_map/ppermute | solution.py:26
  174.8 4.3 %collective-permute-done.23 = bf16[56,2048]{1,0:T(8,128)(2,1)S(1)} collective-permute-done((bf16[56,2048]{1,0:T(8,128)(2,1)S(1)}, bf16[56,2048]{1,0:T(8,128)(2,1)S(1)}, u32[]{:S(2)}, u32[]{:S(2)}) %collective-permute-start.23) | collective-permute-done | bytes 229408 | tf_op jit(solution)/shard_map/ppermute | solution.py:26
  179.0 2.2 collective-permute-done.24
  183.8 11.1 %collective-permute-done.25 = bf16[4,56,2048]{2,1,0:T(8,128)(2,1)S(1)} collective-permute-done((bf16[4,56,2048]{2,1,0:T(8,128)(2,1)S(1)}, bf16[4,56,2048]{2,1,0:T(8,128)(2,1)S(1)}, u32[]{:S(2)}, u32[]{:S(2)}) %collective-permute-start.25) | collective-permute-done | bytes 917536 | tf_op jit(solution)/shard_map/ppermute | solution.py:26
  197.3 7.3 %collective-permute-done.27 = bf16[4,56,1024]{2,1,0:T(8,128)(2,1)S(1)} collective-permute-done((bf16[4,56,1024]{2,1,0:T(8,128)(2,1)S(1)}, bf16[4,56,1024]{2,1,0:T(8,128)(2,1)S(1)}, u32[]{:S(2)}, u32[]{:S(2)}) %collective-permute-start.27) | collective-permute-done | bytes 458784 | tf_op jit(solution)/shard_map/ppermute | solution.py:26
  205.9 2.1 pad_maximum_fusion
  208.0 4.8 %multiply_convert_fusion.1 = bf16[896,448]{0,1:T(8,128)(2,1)S(1)} fusion(bf16[896,2048]{1,0:T(8,128)(2,1)} %bitcast.104, bf16[448,2048]{1,0:T(8,128)(2,1)} %all-gather.2.cloned.1.call-done), kind=kOutput, calls=%fused_computation.18 | convolution fusion | flops 1644969984 | bytes 6307840 | tf_op jit(solution)/shard_map/dot_general | solution.py:261
  212.9 2.1 multiply_convert_fusion
  219.1 25.1 %all_to_all.5 = bf16[4,224,896]{2,1,0:T(8,128)(2,1)S(1)} all-to-all(bf16[4,224,896]{2,1,0:T(8,128)(2,1)S(1)} %bitcast.101), channel_id=1, replica_groups=mesh['y'=4,'zh'=2,'x'=4,'a'=2,'b'=2,'c'=2] {'y'}, dimensions={0} | all-to-all | bytes 3211264 | tf_op jit(solution)/shard_map/all_to_all | solution.py:272
  244.3 2.1 maximum_convert_fusion
  (114 shorter events, 35.3 us)
Async XLA Ops:
  6.5 201.4 %all-gather.2.cloned.1.call-start = ((), (), s32[]{:S(2)}) async-start(), calls=%async_computation.1 | async-start | bytes 2064384 | tf_op jit(solution)/shard_map/all_gather | solution.py:255
  7.5 14.2 %collective-permute-start.2 = (bf16[64,1024]{1,0:T(8,128)(2,1)S(1)}, bf16[64,1024]{1,0:T(8,128)(2,1)S(1)}, u32[]{:S(2)}, u32[]{:S(2)}) collective-permute-start(bf16[64,1024]{1,0:T(8,128)(2,1)S(1)} %get-tuple-element.93), channel_id=1, source_target_pairs={{0,34},{2,32},{32,2},{34,0},{1,35},{3,33},{33,3},{35,1},{4,38},{6,... | collective-permute-start | bytes 393224 | tf_op jit(solution)/shard_map/ppermute | solution.py:26
  7.7 14.1 %collective-permute-start = (bf16[64,1024]{1,0:T(8,128)(2,1)S(1)}, bf16[64,1024]{1,0:T(8,128)(2,1)S(1)}, u32[]{:S(2)}, u32[]{:S(2)}) collective-permute-start(bf16[64,1024]{1,0:T(8,128)(2,1)S(1)} %get-tuple-element.93), channel_id=1, source_target_pairs={{0,2},{2,0},{1,3},{3,1},{4,6},{6,4},{5,7},{7,5},{8,10},{10,8},{9,1... | collective-permute-start | bytes 393224 | tf_op jit(solution)/shard_map/ppermute | solution.py:26
  9.6 12.1 %collective-permute-start.1 = (bf16[64,1024]{1,0:T(8,128)(2,1)S(1)}, bf16[64,1024]{1,0:T(8,128)(2,1)S(1)}, u32[]{:S(2)}, u32[]{:S(2)}) collective-permute-start(bf16[64,1024]{1,0:T(8,128)(2,1)S(1)} %get-tuple-element.94), channel_id=1, source_target_pairs={{0,32},{32,0},{1,33},{33,1},{2,34},{34,2},{3,35},{35,3},{4,36},{36... | collective-permute-start | bytes 393224 | tf_op jit(solution)/shard_map/ppermute | solution.py:26
  22.0 9.7 %collective-permute-start.3 = (bf16[128,2048]{1,0:T(8,128)(2,1)S(1)}, bf16[128,2048]{1,0:T(8,128)(2,1)S(1)}, u32[]{:S(2)}, u32[]{:S(2)}) collective-permute-start(bf16[128,2048]{1,0:T(8,128)(2,1)S(1)} %get-tuple-element.84), channel_id=1, source_target_pairs={{0,8},{1,65},{8,0},{9,73},{16,24},{17,81},{24,16},{25,89},{64,72},... | collective-permute-start | bytes 1572872 | tf_op jit(solution)/shard_map/ppermute | solution.py:26
  23.6 16.0 %collective-permute-start.4 = (bf16[128,2048]{1,0:T(8,128)(2,1)S(1)}, bf16[128,2048]{1,0:T(8,128)(2,1)S(1)}, u32[]{:S(2)}, u32[]{:S(2)}) collective-permute-start(bf16[128,2048]{1,0:T(8,128)(2,1)S(1)} %get-tuple-element.84), channel_id=1, source_target_pairs={{0,24},{1,193},{8,16},{9,201},{16,8},{17,209},{24,0},{25,217},{64,... | collective-permute-start | bytes 1572872 | tf_op jit(solution)/shard_map/ppermute | solution.py:26
  25.7 13.9 %collective-permute-start.5 = (bf16[128,2048]{1,0:T(8,128)(2,1)S(1)}, bf16[128,2048]{1,0:T(8,128)(2,1)S(1)}, u32[]{:S(2)}, u32[]{:S(2)}) collective-permute-start(bf16[128,2048]{1,0:T(8,128)(2,1)S(1)} %get-tuple-element.84), channel_id=1, source_target_pairs={{0,16},{1,129},{8,24},{9,137},{16,0},{17,145},{24,8},{25,153},{64,... | collective-permute-start | bytes 1572872 | tf_op jit(solution)/shard_map/ppermute | solution.py:26
  26.9 20.1 %collective-permute-start.6 = (bf16[896,384]{1,0:T(8,128)(2,1)S(1)}, bf16[896,384]{1,0:T(8,128)(2,1)S(1)}, u32[]{:S(2)}, u32[]{:S(2)}) collective-permute-start(bf16[896,384]{1,0:T(8,128)(2,1)S(1)} %slice.125), channel_id=1, source_target_pairs={{0,2},{2,0},{1,3},{3,1},{4,6},{6,4},{5,7},{7,5},{8,10},{10,8},{9,1... | collective-permute-start | bytes 2064392 | tf_op jit(solution)/shard_map/ppermute | solution.py:26
  39.9 38.1 %copy-start.5 = (bf16[4,128,2048]{2,1,0:T(8,128)(2,1)}, bf16[4,128,2048]{2,1,0:T(8,128)(2,1)S(1)}, u32[]{:S(2)}) copy-start(bf16[4,128,2048]{2,1,0:T(8,128)(2,1)S(1)} %pad_maximum_fusion.1.refs_3_) | copy-start | bytes 6291460
  47.0 29.7 %collective-permute-start.7 = (bf16[4,128,2048]{2,1,0:T(8,128)(2,1)S(1)}, bf16[4,128,2048]{2,1,0:T(8,128)(2,1)S(1)}, u32[]{:S(2)}, u32[]{:S(2)}) collective-permute-start(bf16[4,128,2048]{2,1,0:T(8,128)(2,1)S(1)} %pad_maximum_fusion.1.refs_3_), channel_id=1, source_target_pairs={{0,64},{1,9},{8,72},{9,1},{16,80},{17,25},{24,88},{25,17},{64,0},{... | collective-permute-start | bytes 6291464 | tf_op jit(solution)/shard_map/ppermute | solution.py:26
  47.9 28.8 %collective-permute-start.8 = (bf16[4,128,2048]{2,1,0:T(8,128)(2,1)S(1)}, bf16[4,128,2048]{2,1,0:T(8,128)(2,1)S(1)}, u32[]{:S(2)}, u32[]{:S(2)}) collective-permute-start(bf16[4,128,2048]{2,1,0:T(8,128)(2,1)S(1)} %pad_maximum_fusion.1.refs_3_), channel_id=1, source_target_pairs={{0,192},{1,25},{8,200},{9,17},{16,208},{17,9},{24,216},{25,1},{64,... | collective-permute-start | bytes 6291464 | tf_op jit(solution)/shard_map/ppermute | solution.py:26
  50.2 26.5 %collective-permute-start.9 = (bf16[896,640]{1,0:T(8,128)(2,1)S(1)}, bf16[896,640]{1,0:T(8,128)(2,1)S(1)}, u32[]{:S(2)}, u32[]{:S(2)}) collective-permute-start(bf16[896,640]{1,0:T(8,128)(2,1)S(1)} %slice.126), channel_id=1, source_target_pairs={{0,2},{2,0},{1,3},{3,1},{4,6},{6,4},{5,7},{7,5},{8,10},{10,8},{9,1... | collective-permute-start | bytes 3440648 | tf_op jit(solution)/shard_map/ppermute | solution.py:26
  78.0 16.9 %collective-permute-start.11 = (bf16[2,128,2048]{2,1,0:T(8,128)(2,1)}, bf16[2,128,2048]{2,1,0:T(8,128)(2,1)}, u32[]{:S(2)}, u32[]{:S(2)}) collective-permute-start(bf16[2,128,2048]{2,1,0:T(8,128)(2,1)} %slice.96), channel_id=1, source_target_pairs={{0,192},{1,25},{8,200},{9,17},{16,208},{17,9},{24,216},{25,1},{64,... | collective-permute-start | bytes 3145736 | tf_op jit(solution)/shard_map/ppermute | solution.py:26
  80.7 15.1 %collective-permute-start.12 = (bf16[2,128,2048]{2,1,0:T(8,128)(2,1)}, bf16[2,128,2048]{2,1,0:T(8,128)(2,1)}, u32[]{:S(2)}, u32[]{:S(2)}) collective-permute-start(bf16[2,128,2048]{2,1,0:T(8,128)(2,1)} %slice.97), channel_id=1, source_target_pairs={{0,64},{1,9},{8,72},{9,1},{16,80},{17,25},{24,88},{25,17},{64,0},{... | collective-permute-start | bytes 3145736 | tf_op jit(solution)/shard_map/ppermute | solution.py:26
  88.6 6.4 %collective-permute-start.10 = (bf16[4,2,224,128]{3,2,1,0:T(8,128)(2,1)S(1)}, bf16[4,2,224,128]{3,2,1,0:T(8,128)(2,1)}, u32[]{:S(2)}, u32[]{:S(2)}) collective-permute-start(bf16[4,2,224,128]{3,2,1,0:T(8,128)(2,1)S(1)} %get-tuple-element.41), channel_id=1, source_target_pairs={{0,1},{1,0},{2,3},{3,2},{4,5},{5,4},{6,7},{7,6},{8,9},{9,8},{10,11... | collective-permute-start | bytes 1376264 | tf_op jit(solution)/shard_map/ppermute | solution.py:26
  95.8 15.1 %collective-permute-start.13 = (bf16[5,2,224,128]{3,2,1,0:T(8,128)(2,1)S(1)}, bf16[5,2,224,128]{3,2,1,0:T(8,128)(2,1)S(1)}, u32[]{:S(2)}, u32[]{:S(2)}) collective-permute-start(bf16[5,2,224,128]{3,2,1,0:T(8,128)(2,1)S(1)} %get-tuple-element.47), channel_id=1, source_target_pairs={{0,1},{1,0},{2,3},{3,2},{4,5},{5,4},{6,7},{7,6},{8,9},{9,8},{10,11... | collective-permute-start | bytes 1720328 | tf_op jit(solution)/shard_map/ppermute | solution.py:26
  97.0 13.9 %collective-permute-start.14 = (bf16[4,2,112,128]{3,2,1,0:T(8,128)(2,1)S(1)}, bf16[4,2,112,128]{3,2,1,0:T(8,128)(2,1)S(1)}, u32[]{:S(2)}, u32[]{:S(2)}) collective-permute-start(bf16[4,2,112,128]{3,2,1,0:T(8,128)(2,1)S(1)} %fusion.2), channel_id=1, source_target_pairs={{0,4},{4,0},{1,5},{5,1},{2,6},{6,2},{3,7},{7,3},{8,12},{12,8},{9,1... | collective-permute-start | bytes 688136 | tf_op jit(solution)/shard_map/ppermute | solution.py:26
  110.9 2.3 collective-permute-start.15
  111.1 14.9 %collective-permute-start.16 = (bf16[5,2,112,128]{3,2,1,0:T(8,128)(2,1)S(1)}, bf16[5,2,112,128]{3,2,1,0:T(8,128)(2,1)S(1)}, u32[]{:S(2)}, u32[]{:S(2)}) collective-permute-start(bf16[5,2,112,128]{3,2,1,0:T(8,128)(2,1)S(1)} %fusion.1), channel_id=1, source_target_pairs={{0,4},{4,0},{1,5},{5,1},{2,6},{6,2},{3,7},{7,3},{8,12},{12,8},{9,1... | collective-permute-start | bytes 860168 | tf_op jit(solution)/shard_map/ppermute | solution.py:26
  126.2 12.3 %collective-permute-start.17 = (bf16[7,2,56,128]{3,2,1,0:T(8,128)(2,1)S(1)}, bf16[7,2,56,128]{3,2,1,0:T(8,128)(2,1)S(1)}, u32[]{:S(2)}, u32[]{:S(2)}) collective-permute-start(bf16[7,2,56,128]{3,2,1,0:T(8,128)(2,1)S(1)} %get-tuple-element.90), channel_id=1, source_target_pairs={{0,4},{4,0},{1,5},{5,1},{2,6},{6,2},{3,7},{7,3},{8,12},{12,8},{9,1... | collective-permute-start | bytes 602120 | tf_op jit(solution)/shard_map/ppermute | solution.py:26
  139.4 13.7 %collective-permute-start.18 = (bf16[56,2048]{1,0:T(8,128)(2,1)S(1)}, bf16[56,2048]{1,0:T(8,128)(2,1)S(1)}, u32[]{:S(2)}, u32[]{:S(2)}) collective-permute-start(bf16[56,2048]{1,0:T(8,128)(2,1)S(1)} %shard_map.49), channel_id=1, source_target_pairs={{2,0},{3,1},{6,4},{7,5},{10,8},{11,9},{14,12},{15,13},{18,16},{19,... | collective-permute-start | bytes 688136 | tf_op jit(solution)/shard_map/ppermute | solution.py:26
  140.7 10.7 %collective-permute-start.19 = (bf16[7,2,56,128]{3,2,1,0:T(8,128)(2,1)S(1)}, bf16[7,2,56,128]{3,2,1,0:T(8,128)(2,1)S(1)}, u32[]{:S(2)}, u32[]{:S(2)}) collective-permute-start(bf16[7,2,56,128]{3,2,1,0:T(8,128)(2,1)S(1)} %get-tuple-element.89), channel_id=1, source_target_pairs={{0,4},{4,0},{1,5},{5,1},{2,6},{6,2},{3,7},{7,3},{8,12},{12,8},{9,1... | collective-permute-start | bytes 602120 | tf_op jit(solution)/shard_map/ppermute | solution.py:26
  143.2 12.9 %collective-permute-start.20 = (bf16[56,2048]{1,0:T(8,128)(2,1)S(1)}, bf16[56,2048]{1,0:T(8,128)(2,1)S(1)}, u32[]{:S(2)}, u32[]{:S(2)}) collective-permute-start(bf16[56,2048]{1,0:T(8,128)(2,1)S(1)} %shard_map.49), channel_id=1, source_target_pairs={{0,0},{4,16},{8,2},{12,18},{16,4},{20,20},{24,6},{28,22},{1,1},{5,... | collective-permute-start | bytes 688136 | tf_op jit(solution)/shard_map/ppermute | solution.py:26
  152.4 1.4 collective-permute-start.21
  156.2 18.6 %collective-permute-start.22 = (bf16[56,2048]{1,0:T(8,128)(2,1)S(1)}, bf16[56,2048]{1,0:T(8,128)(2,1)S(1)}, u32[]{:S(2)}, u32[]{:S(2)}) collective-permute-start(bf16[56,2048]{1,0:T(8,128)(2,1)S(1)} %broadcast_select_fusion.6), channel_id=1, source_target_pairs={{0,8},{1,65},{8,0},{9,73},{16,24},{17,81},{24,16},{25,89},{64,72},... | collective-permute-start | bytes 688136 | tf_op jit(solution)/shard_map/ppermute | solution.py:26
  167.3 11.8 %collective-permute-start.23 = (bf16[56,2048]{1,0:T(8,128)(2,1)S(1)}, bf16[56,2048]{1,0:T(8,128)(2,1)S(1)}, u32[]{:S(2)}, u32[]{:S(2)}) collective-permute-start(bf16[56,2048]{1,0:T(8,128)(2,1)S(1)} %broadcast_select_fusion.6), channel_id=1, source_target_pairs={{0,24},{1,193},{8,16},{9,201},{16,8},{17,209},{24,0},{25,217},{64,... | collective-permute-start | bytes 688136 | tf_op jit(solution)/shard_map/ppermute | solution.py:26
  173.4 7.8 %collective-permute-start.24 = (bf16[56,2048]{1,0:T(8,128)(2,1)S(1)}, bf16[56,2048]{1,0:T(8,128)(2,1)S(1)}, u32[]{:S(2)}, u32[]{:S(2)}) collective-permute-start(bf16[56,2048]{1,0:T(8,128)(2,1)S(1)} %broadcast_select_fusion.6), channel_id=1, source_target_pairs={{0,16},{1,129},{8,24},{9,137},{16,0},{17,145},{24,8},{25,153},{64,... | collective-permute-start | bytes 688136 | tf_op jit(solution)/shard_map/ppermute | solution.py:26
  181.4 13.5 %collective-permute-start.25 = (bf16[4,56,2048]{2,1,0:T(8,128)(2,1)S(1)}, bf16[4,56,2048]{2,1,0:T(8,128)(2,1)S(1)}, u32[]{:S(2)}, u32[]{:S(2)}) collective-permute-start(bf16[4,56,2048]{2,1,0:T(8,128)(2,1)S(1)} %get-tuple-element.74), channel_id=1, source_target_pairs={{0,64},{1,9},{8,72},{9,1},{16,80},{17,25},{24,88},{25,17},{64,0},{... | collective-permute-start | bytes 2752520 | tf_op jit(solution)/shard_map/ppermute | solution.py:26
  182.6 14.6 %collective-permute-start.26 = (bf16[4,56,2048]{2,1,0:T(8,128)(2,1)S(1)}, bf16[4,56,2048]{2,1,0:T(8,128)(2,1)S(1)}, u32[]{:S(2)}, u32[]{:S(2)}) collective-permute-start(bf16[4,56,2048]{2,1,0:T(8,128)(2,1)S(1)} %get-tuple-element.74), channel_id=1, source_target_pairs={{0,192},{1,25},{8,200},{9,17},{16,208},{17,9},{24,216},{25,1},{64,... | collective-permute-start | bytes 2752520 | tf_op jit(solution)/shard_map/ppermute | solution.py:26
  194.9 9.8 %collective-permute-start.27 = (bf16[4,56,1024]{2,1,0:T(8,128)(2,1)S(1)}, bf16[4,56,1024]{2,1,0:T(8,128)(2,1)S(1)}, u32[]{:S(2)}, u32[]{:S(2)}) collective-permute-start(bf16[4,56,1024]{2,1,0:T(8,128)(2,1)S(1)} %slice.135), channel_id=1, source_target_pairs={{0,192},{1,25},{8,200},{9,17},{16,208},{17,9},{24,216},{25,1},{64,... | collective-permute-start | bytes 1376264 | tf_op jit(solution)/shard_map/ppermute | solution.py:26
  197.2 8.6 %collective-permute-start.28 = (bf16[4,56,1024]{2,1,0:T(8,128)(2,1)S(1)}, bf16[4,56,1024]{2,1,0:T(8,128)(2,1)S(1)}, u32[]{:S(2)}, u32[]{:S(2)}) collective-permute-start(bf16[4,56,1024]{2,1,0:T(8,128)(2,1)S(1)} %slice.136), channel_id=1, source_target_pairs={{0,64},{1,9},{8,72},{9,1},{16,80},{17,25},{24,88},{25,17},{64,0},{... | collective-permute-start | bytes 1376264 | tf_op jit(solution)/shard_map/ppermute | solution.py:26
  208.0 4.9 %collective-permute-start.29 = (bf16[448,2048]{1,0:T(8,128)(2,1)}, bf16[448,2048]{1,0:T(8,128)(2,1)S(1)}, u32[]{:S(2)}, u32[]{:S(2)}) collective-permute-start(bf16[448,2048]{1,0:T(8,128)(2,1)} %all-gather.2.cloned.1.call-done), channel_id=1, source_target_pairs={{0,1},{1,0},{2,3},{3,2},{4,5},{5,4},{6,7},{7,6},{8,9},{9,8},{10,11... | collective-permute-start | bytes 5505032 | tf_op jit(solution)/shard_map/ppermute | solution.py:26
  (9 other events, 65.6 us)
Sparse Core Ops, SparseCore 0:
  156.3 50.8 all-gather.1
